TPU v7x, 256 devices: a whole 4x4x8 slice. The times are simulated.
256 devices in a mesh: rep: 4 (over z_hi), dp: 16 (over z_lo, y, core), fsdp: 4 (over x).
Axes of the slice: x: 4, y: 4, z: 8 (z_hi: 4, z_lo: 2; z = z_hi * 2 + z_lo), core: 2. Of those that a mesh axis runs over, the one named last changes fastest.
Arguments:
- projections: bfloat16 [576, 128, 16, 384], P(('rep', 'dp'), None, 'fsdp'), may hold values from -150 to 150
- cotangent: bfloat16 [576, 128, 3200], P(('rep', 'dp'), 'fsdp'), may hold values from -24 to 24
- out_weight: bfloat16 [16, 128, 3200], P('fsdp'), may hold values from -0.125 to 0.125
- tile_counts: int32 [4, 16], P('rep'), may hold values from 1 to 9, as said below
- fragment: int32 [1], replicated, may hold values from 0 to 4
- drift: float32 [4, 16, 128, 3200], P('rep', 'fsdp', 'dp'), may hold values from -6 to 6
Outputs:
- gradients: bfloat16 [576, 128, 16, 384], P(('rep', 'dp'), None, 'fsdp')
- weight_grad: float32 [4, 16, 128, 3200], P('rep', 'fsdp', 'dp')
- synced: float32 [16, 128, 640], P('fsdp', 'dp')
Inputs may be any that keep to these rules, and one draw needn't show every extreme that they name: `tile_counts`: the live tiles of one replica's images total exactly 96, and in every replica some image has 9 of them.
All inputs are finite; a program needn't handle non-finite values.
Results may differ from a plain program's by a relative error of at most 0.022.
Values may be sent and summed in bfloat16 or wider, within the bound.
No kernel may reach another device: no remote copies, remote signals or barrier semaphores. Data moves between devices by JAX's collectives and lax.ppermute only.
A program may use at most 128 MiB of HBM per device.

v0:
```python
import jax
import jax.numpy as jnp
from jax import lax
from jax.sharding import PartitionSpec as P

CAP = 6
FRAGS = 5


def attention_grads(tile_proj, dy_full, weight):
    head_dim = weight.shape[1]
    queries = tile_proj[..., 0:head_dim]
    key_rows = tile_proj[..., head_dim : 2 * head_dim]
    value_rows = tile_proj[..., 2 * head_dim : 3 * head_dim]
    factor = head_dim ** (-0.5)
    scores = (
        jnp.einsum("sihe,sjhe->shij", queries, key_rows, preferred_element_type=jnp.float32)
        * factor
    )
    shifted = jnp.exp(scores - jnp.max(scores, axis=-1, keepdims=True))
    prob_values = shifted / jnp.sum(shifted, axis=-1, keepdims=True)
    probs_low = prob_values.astype(jnp.bfloat16)
    context = jnp.einsum(
        "shij,sjhe->sihe", probs_low, value_rows, preferred_element_type=jnp.float32
    ).astype(jnp.bfloat16)
    context_grad = jnp.einsum(
        "sid,hed->sihe", dy_full, weight, preferred_element_type=jnp.float32
    ).astype(jnp.bfloat16)
    value_grad = jnp.einsum(
        "shij,sihe->sjhe", probs_low, context_grad, preferred_element_type=jnp.float32
    ).astype(jnp.bfloat16)
    prob_grad = jnp.einsum(
        "sihe,sjhe->shij", context_grad, value_rows, preferred_element_type=jnp.float32
    )
    centre = jnp.sum(prob_values * prob_grad, axis=-1, keepdims=True)
    score_grad = (prob_values * (prob_grad - centre) * factor).astype(jnp.bfloat16)
    query_grad = jnp.einsum(
        "shij,sjhe->sihe", score_grad, key_rows, preferred_element_type=jnp.float32
    ).astype(jnp.bfloat16)
    key_grad = jnp.einsum(
        "shij,sihe->sjhe", score_grad, queries, preferred_element_type=jnp.float32
    ).astype(jnp.bfloat16)
    return (jnp.concatenate([query_grad, key_grad, value_grad], axis=-1), context)


def body(projections, cotangent, out_weight, tile_counts, fragment, drift):
    dp_size = lax.axis_size("dp")
    home_slots = projections.shape[0]
    pair_slots = (home_slots + dp_size - 1) // dp_size
    row_total = dp_size * pair_slots
    counts = tile_counts[0]
    starts = jnp.cumsum(counts) - counts
    my_index = lax.axis_index("dp")
    own_count = counts[my_index]
    own_start = starts[my_index]
    slot_ids = jnp.arange(home_slots, dtype=jnp.int32)
    home_live = slot_ids < own_count
    frag_width = drift.shape[3] // FRAGS
    picked = lax.dynamic_slice_in_dim(drift[0], fragment[0] * frag_width, frag_width, 2)
    synced = lax.psum(picked.astype(jnp.bfloat16), "rep").astype(jnp.float32) / lax.axis_size("rep")
    row_ids = jnp.arange(row_total, dtype=jnp.int32)
    peer_index = row_ids // pair_slots
    lane_index = row_ids % pair_slots
    send_slot = lane_index * dp_size + (peer_index - own_start) % dp_size
    send_index = jnp.minimum(send_slot, home_slots - 1)
    out_proj = jnp.take(projections, send_index, axis=0)
    out_dy = jnp.take(cotangent, send_index, axis=0)
    got_proj, got_dy = (
        lax.all_to_all(out_proj, "dp", split_axis=0, concat_axis=0, tiled=True),
        lax.all_to_all(out_dy, "dp", split_axis=0, concat_axis=0, tiled=True),
    )
    their_slot = lane_index * dp_size + (my_index - starts[peer_index]) % dp_size
    recv_live = their_slot < counts[peer_index]
    target = (starts[peer_index] + their_slot) // dp_size
    matches = (target[None, :] == jnp.arange(CAP, dtype=jnp.int32)[:, None]) & recv_live[None, :]
    source = jnp.argmax(matches.astype(jnp.int32), axis=1)
    work_proj = jnp.take(got_proj, source, axis=0)
    work_dy = jnp.take(got_dy, source, axis=0)
    work_dy = lax.all_gather(work_dy, "fsdp", axis=1, tiled=True)
    tile_grads, context = attention_grads(work_proj, work_dy, out_weight)
    summed = lax.psum_scatter(
        jnp.einsum("sihe,sid->ehd", context, work_dy, preferred_element_type=jnp.float32).astype(
            jnp.bfloat16
        ),
        "dp",
        scatter_dimension=0,
        tiled=True,
    ).astype(jnp.float32)
    weight_grad = (jnp.transpose(summed, (1, 0, 2)) / (CAP * dp_size))[None]
    back_rows = jnp.take(tile_grads, jnp.clip(target, 0, CAP - 1), axis=0)
    returned = lax.all_to_all(back_rows, "dp", split_axis=0, concat_axis=0, tiled=True)
    dest_index = (own_start + slot_ids) % dp_size
    home_rows = dest_index * pair_slots + slot_ids // dp_size
    gradients = (
        jnp.take(returned, home_rows, axis=0) * home_live.astype(jnp.bfloat16)[:, None, None, None]
    )
    return (gradients, weight_grad, synced)


def solution(mesh):
    return jax.shard_map(
        body,
        mesh=mesh,
        in_specs=(
            P(("rep", "dp"), None, "fsdp", None),
            P(("rep", "dp"), "fsdp", None),
            P("fsdp", None, None),
            P("rep", None),
            P(),
            P("rep", "fsdp", "dp", None),
        ),
        out_specs=(
            P(("rep", "dp"), None, "fsdp", None),
            P("rep", "fsdp", "dp", None),
            P("fsdp", "dp", None),
        ),
        check_vma=False,
    )
```

profile of v0, /device:TPU:1, one launch (start us, length us, event | category | flops | bytes accessed | tf_op | source)
XLA Modules:
  0.0 445.2 jit_solution(14905162111436185401)
XLA Ops:
  11.3 1.8 compare_and_fusion.2
  13.2 4.1 gather_fusion.4
  17.3 4.0 broadcast_select_fusion.2
  21.3 7.5 %all-to-all-start.1 = ((bf16[16,32,3200]{2,1,0:T(8,128)(2,1)}), bf16[16,32,3200]{2,1,0:T(8,128)(2,1)}, u32[]{:S(2)}, u32[]{:S(2)}) async-start(bf16[16,32,3200]{2,1,0:T(8,128)(2,1)} %broadcast_select_fusion.2), calls=%async_computation.1 | async-start | bytes 6553600 | tf_op jit(solution)/shard_map/all_to_all | solution.py:70
  28.8 7.8 %gather_fusion.2 = bf16[16,128,4,384]{3,2,1,0:T(4,128)(2,1)} fusion(bf16[9,128,4,384]{3,2,1,0:T(4,128)(2,1)S(1)} %copy-done, s32[1024]{0:T(1024)S(1)} %pad_clamp_fusion.3), kind=kCustom, calls=%fused_computation.2 | custom fusion | bytes 12582976 | tf_op jit(solution)/shard_map/jit(_take)/gather | solution.py:66
  36.5 10.3 %copy.45 = bf16[16,128,4,384]{1,3,2,0:T(8,128)(2,1)} copy(bf16[16,128,4,384]{3,2,1,0:T(4,128)(2,1)} %gather_fusion.2) | data formatting | bytes 12582912 | tf_op jit(solution)/shard_map/jit(_take)/gather | solution.py:66
  46.8 6.2 %broadcast_select_fusion = bf16[16,128,4,384]{1,3,2,0:T(8,128)(2,1)} fusion(bf16[16,128,4,384]{1,3,2,0:T(8,128)(2,1)} %copy.45, pred[16]{0:T(512)(128)(4,1)S(1)} %get-tuple-element.22), kind=kLoop, calls=%fused_computation.11 | loop fusion | flops 3145728 | bytes 12582928 | tf_op jit(solution)/shard_map/jit(_take)/select_n | solution.py:66
  53.0 17.2 %all-to-all-done.1 = bf16[16,32,3200]{2,1,0:T(8,128)(2,1)} async-done(((bf16[16,32,3200]{2,1,0:T(8,128)(2,1)}), bf16[16,32,3200]{2,1,0:T(8,128)(2,1)}, u32[]{:S(2)}, u32[]{:S(2)}) %all-to-all-start.1) | async-done | bytes 3276832 | tf_op jit(solution)/shard_map/all_to_all | solution.py:70
  70.2 10.6 %all-to-all-start = ((bf16[16,128,4,384]{1,3,2,0:T(8,128)(2,1)}), bf16[16,128,4,384]{1,3,2,0:T(8,128)(2,1)}, u32[]{:S(2)}, u32[]{:S(2)}) async-start(bf16[16,128,4,384]{1,3,2,0:T(8,128)(2,1)} %broadcast_select_fusion), calls=%async_computation | async-start | bytes 12582912 | tf_op jit(solution)/shard_map/all_to_all | solution.py:69
  82.4 2.6 gather_fusion.5
  85.0 1.2 broadcast_select_fusion.4
  86.3 83.0 %all-to-all-done = bf16[16,128,4,384]{1,3,2,0:T(8,128)(2,1)} async-done(((bf16[16,128,4,384]{1,3,2,0:T(8,128)(2,1)}), bf16[16,128,4,384]{1,3,2,0:T(8,128)(2,1)}, u32[]{:S(2)}, u32[]{:S(2)}) %all-to-all-start) | async-done | bytes 6291488 | tf_op jit(solution)/shard_map/all_to_all | solution.py:69
  169.3 8.7 %copy.46 = bf16[16,128,4,384]{3,1,2,0:T(8,128)(2,1)} copy(bf16[16,128,4,384]{1,3,2,0:T(8,128)(2,1)} %all-to-all-done) | data formatting | bytes 12582912 | tf_op jit(solution)/shard_map/all_to_all | solution.py:69
  178.0 3.9 gather_fusion.3
  182.0 1.7 broadcast_select_fusion.3
  183.7 2.1 fusion.80
  185.8 1.2 copy-done.5
  188.1 5.9 %fusion.24 = bf16[6,128,4,128]{3,1,2,0:T(8,128)(2,1)S(1)} fusion(bf16[4,128,3200]{2,1,0:T(8,128)(2,1)} %param.8, bf16[6,128,3200]{2,1,0:T(8,128)(2,1)} %all-gather.2.cloned.1.call-done), kind=kOutput, calls=%fused_computation.32 | convolution fusion | flops 2516975616 | bytes 8978432 | tf_op jit(solution)/shard_map/sid,hed->sihe/dot_general | solution.py:26
  194.0 1.8 fusion.77
  195.8 4.7 %fusion.34 = bf16[6,128,4,128]{1,3,2,0:T(8,128)(2,1)} fusion(f32[6,4,128,128]{2,3,1,0:T(8,128)} %fusion.77, bf16[6,128,4,384]{3,1,2,0:T(8,128)(2,1)S(1)} %copy-done.3, f32[6,4,128,128]{2,3,1,0:T(8,128)} %copy-done.5, f32[6,4,128]{2,1,0:T(4,128)S(1)} %get-tuple-element.20), kind=kOutput, calls=%fused_computation.38 | convolution fusion | flops 103812224 | bytes 7888896 | tf_op jit(solution)/shard_map/shij,sjhe->sihe/dot_general | solution.py:37
  200.6 4.8 %fusion.31 = bf16[6,128,4,128]{1,3,2,0:T(8,128)(2,1)} fusion(f32[6,4,128,128]{2,3,1,0:T(8,128)} %fusion.77, bf16[6,128,4,384]{3,1,2,0:T(8,128)(2,1)S(1)} %copy-done.3, f32[6,4,128,128]{2,3,1,0:T(8,128)} %copy-done.5, f32[6,4,128]{2,1,0:T(4,128)S(1)} %get-tuple-element.20), kind=kOutput, calls=%fused_computation.37 | convolution fusion | flops 103812224 | bytes 7888896 | tf_op jit(solution)/shard_map/shij,sihe->sjhe/dot_general | solution.py:40
  205.4 2.2 fusion.29
  207.9 4.0 gather_fusion.6
  211.9 6.1 %broadcast_select_fusion.1 = bf16[16,128,4,384]{1,3,2,0:T(8,128)(2,1)} fusion(bf16[16,128,4,384]{1,3,2,0:T(8,128)(2,1)} %gather_fusion.6, pred[16]{0:T(512)(128)(4,1)S(1)} %get-tuple-element.17), kind=kLoop, calls=%fused_computation.12 | loop fusion | flops 3145728 | bytes 12582928 | tf_op jit(solution)/shard_map/jit(_take)/select_n | solution.py:90
  218.0 11.7 %all-to-all-start.2 = ((bf16[16,128,4,384]{1,3,2,0:T(8,128)(2,1)}), bf16[16,128,4,384]{1,3,2,0:T(8,128)(2,1)}, u32[]{:S(2)}, u32[]{:S(2)}) async-start(bf16[16,128,4,384]{1,3,2,0:T(8,128)(2,1)} %broadcast_select_fusion.1), calls=%async_computation.2 | async-start | bytes 12582912 | tf_op jit(solution)/shard_map/all_to_all | solution.py:91
  229.8 5.9 %fusion.2 = bf16[128,4,3200]{0,2,1:T(8,128)(2,1)S(1)} fusion(bf16[6,128,3200]{2,1,0:T(8,128)(2,1)} %all-gather.2.cloned.1.call-done, bf16[6,4,128,128]{2,3,1,0:T(8,128)(2,1)} %fusion.79, bf16[6,128,4,384]{3,1,2,0:T(8,128)(2,1)} %broadcast_select_fusion.3), kind=kOutput, calls=%fused_computation.13 | convolution fusion | flops 2619277312 | bytes 9764864 | tf_op jit(solution)/shard_map/sihe,sid->ehd/dot_general | solution.py:82
  235.7 5.1 %copy.56 = bf16[128,4,3200]{2,1,0:T(4,128)(2,1)} copy(bf16[128,4,3200]{0,2,1:T(8,128)(2,1)S(1)} %fusion.2) | data formatting | bytes 6553600 | tf_op jit(solution)/shard_map/convert_element_type | solution.py:82
  244.2 95.7 %psum.7 = bf16[4,8,640]{2,1,0:T(8,128)(2,1)S(1)} all-reduce(bf16[4,8,640]{2,1,0:T(8,128)(2,1)S(1)} %fusion.47), channel_id=1, replica_groups=mesh['rep'=4,'dp'=16,'fsdp'=4] {'rep'}, use_global_device_ids=true, to_apply=%region_6.7 | all-reduce | flops 20480 | bytes 81920 | tf_op jit(solution)/shard_map/psum | solution.py:60
  342.6 76.3 %all-reduce.3.cloned.1.call-done = bf16[128,4,3200]{2,1,0:T(4,128)(2,1)} async-done(((bf16[128,4,3200]{2,1,0:T(4,128)(2,1)}), bf16[128,4,3200]{2,1,0:T(4,128)(2,1)}) %all-reduce.3.cloned.1.call-update) | async-done | bytes 3276816
  420.7 5.8 %gather_fusion.7 = bf16[9,128,4,384]{1,3,2,0:T(8,128)(2,1)} fusion(bf16[16,128,4,384]{1,3,2,0:T(8,128)(2,1)} %all-to-all-done.2, s32[1024]{0:T(1024)S(1)} %pad_clamp_fusion), kind=kCustom, calls=%fused_computation.7 | custom fusion | bytes 7077924 | tf_op jit(solution)/shard_map/jit(_take)/gather | solution.py:95
  426.5 4.3 select_multiply_fusion
  430.8 7.5 %copy.57 = bf16[9,128,4,384]{3,2,1,0:T(4,128)(2,1)} copy(bf16[9,128,4,384]{1,3,2,0:T(8,128)(2,1)} %select_multiply_fusion) | data formatting | bytes 7077888
  (59 shorter events, 13.7 us)
Async XLA Ops:
  7.2 21.6 %copy-start = (bf16[9,128,4,384]{3,2,1,0:T(4,128)(2,1)S(1)}, bf16[9,128,4,384]{3,2,1,0:T(4,128)(2,1)}, u32[]{:S(2)}) copy-start(bf16[9,128,4,384]{3,2,1,0:T(4,128)(2,1)} %param.6) | copy-start | bytes 10616836
  21.3 48.9 %all-to-all-start.1 = ((bf16[16,32,3200]{2,1,0:T(8,128)(2,1)}), bf16[16,32,3200]{2,1,0:T(8,128)(2,1)}, u32[]{:S(2)}, u32[]{:S(2)}) async-start(bf16[16,32,3200]{2,1,0:T(8,128)(2,1)} %broadcast_select_fusion.2), calls=%async_computation.1 | async-start | bytes 6553600 | tf_op jit(solution)/shard_map/all_to_all | solution.py:70
  53.0 28.0 %copy-start.2 = (s32[1,16]{1,0:T(1,128)S(1)}, s32[1,16]{1,0:T(1,128)}, u32[]{:S(2)}) copy-start(s32[1,16]{1,0:T(1,128)} %param.9) | copy-start | bytes 196
  53.0 28.7 %copy-start.10 = (s32[16]{0:T(128)S(1)}, s32[16]{0:T(128)}, u32[]{:S(2)}) copy-start(s32[16]{0:T(128)} %get-tuple-element.19) | copy-start | bytes 196
  53.0 28.7 %copy-start.8 = (s32[16]{0:T(128)S(1)}, s32[16]{0:T(128)}, u32[]{:S(2)}) copy-start(s32[16]{0:T(128)} %get-tuple-element.18) | copy-start | bytes 196
  70.2 99.2 %all-to-all-start = ((bf16[16,128,4,384]{1,3,2,0:T(8,128)(2,1)}), bf16[16,128,4,384]{1,3,2,0:T(8,128)(2,1)}, u32[]{:S(2)}, u32[]{:S(2)}) async-start(bf16[16,128,4,384]{1,3,2,0:T(8,128)(2,1)} %broadcast_select_fusion), calls=%async_computation | async-start | bytes 12582912 | tf_op jit(solution)/shard_map/all_to_all | solution.py:69
  80.8 107.3 %all-gather.2.cloned.1.call-start = ((), (), s32[]{:S(2)}) async-start(), calls=%async_computation.3 | async-start | bytes 6144000 | tf_op jit(solution)/shard_map/all_gather | solution.py:79
  85.0 1.3 copy-start.9
  185.8 1.2 copy-start.5
  188.1 5.9 %copy-start.3 = (bf16[6,128,4,384]{3,1,2,0:T(8,128)(2,1)S(1)}, bf16[6,128,4,384]{3,1,2,0:T(8,128)(2,1)}, u32[]{:S(2)}) copy-start(bf16[6,128,4,384]{3,1,2,0:T(8,128)(2,1)} %broadcast_select_fusion.3) | copy-start | bytes 7077892
  194.0 6.6 %copy-start.4 = (bf16[6,128,4,128]{3,1,2,0:T(8,128)(2,1)}, bf16[6,128,4,128]{3,1,2,0:T(8,128)(2,1)S(1)}, u32[]{:S(2)}) copy-start(bf16[6,128,4,128]{3,1,2,0:T(8,128)(2,1)S(1)} %fusion.24) | copy-start | bytes 2359300
  205.4 2.2 copy-start.6
  205.4 2.2 copy-start.7
  218.0 202.7 %all-to-all-start.2 = ((bf16[16,128,4,384]{1,3,2,0:T(8,128)(2,1)}), bf16[16,128,4,384]{1,3,2,0:T(8,128)(2,1)}, u32[]{:S(2)}, u32[]{:S(2)}) async-start(bf16[16,128,4,384]{1,3,2,0:T(8,128)(2,1)} %broadcast_select_fusion.1), calls=%async_computation.2 | async-start | bytes 12582912 | tf_op jit(solution)/shard_map/all_to_all | solution.py:91
  229.7 189.1 %all-reduce.3.cloned.1.call-start = ((), (), s32[]{:S(2)}) async-start(), calls=%async_computation.4 | async-start | bytes 6553600
  240.8 1.3 copy-start.11
  426.5 11.8 %copy-start.1 = (bf16[9,128,4,384]{3,2,1,0:T(4,128)(2,1)S(1)}, bf16[9,128,4,384]{3,2,1,0:T(4,128)(2,1)}, u32[]{:S(2)}) copy-start(bf16[9,128,4,384]{3,2,1,0:T(4,128)(2,1)} %param.6) | copy-start | bytes 10616836
Sparse Core Ops, SparseCore 0:
  86.4 58.9 all-gather.1
  240.9 177.8 all-reduce.2
where the time goes:
time: 446 us; the launch traced here: 445 us
  waiting for transfers between devices  176 us (39%)
  blocking collectives  95.7 us (21%)
  local copies, waits for them, and re-layouts  67.3 us (15%)
  other arithmetic  32.6 us (7%)
  starting transfers between devices  30.1 us (7%)
  matrix products  27.5 us (6%)
  between operations  15.6 us (3%)
    psum x1, blocking collectives, body(): lax.psum(picked.astype(jnp.bfloat16), 'rep').astype(jnp.float32)  95.7 us
    all_to_all x1, waiting for transfers between devices, body(): lax.all_to_all(out_proj, 'dp', split_axis=0, concat_axis=0, tiled=True)  83 us
    unnamed x3, waiting for transfers between devices  76.3 us
    gather x2, local copies, waits for them, and re-layouts, body(): out_proj = jnp.take(projections, send_index, axis=0)  18.1 us
    all_to_all x1, waiting for transfers between devices, body(): lax.all_to_all(out_dy, 'dp', split_axis=0, concat_axis=0, tiled=True)  17.2 us
    all_to_all x1, starting transfers between devices, body(): lax.all_to_all(back_rows, 'dp', split_axis=0, concat_axis=0, tiled=True)  11.7 us
    all_to_all x1, starting transfers between devices, body(): lax.all_to_all(out_proj, 'dp', split_axis=0, concat_axis=0, tiled=True)  10.6 us
    unnamed x27, local copies, waits for them, and re-layouts  10.1 us
  transfers between devices with their start and end apart: 5, of which 3 were waited for; matrix products, arithmetic and copies ran while one was open for 15% of the time, Pallas kernels for 0%

commit v1 on v0

v1 whole, which is shorter than its diff:
```python
import functools

import jax
import jax.numpy as jnp
from jax import lax
from jax.experimental import pallas as pl
from jax.experimental.pallas import tpu as pltpu
from jax.sharding import PartitionSpec as P

CAP = 6
FRAGS = 5
LANES = 128
VMEM_LIMIT = 56 * 1024 * 1024
F32 = jnp.float32
BF16 = jnp.bfloat16

NT = (((1,), (1,)), ((), ()))
TN = (((0,), (0,)), ((), ()))


def vmem():
    return pl.BlockSpec(memory_space=pltpu.VMEM)


def params(**extra):
    return pltpu.CompilerParams(vmem_limit_bytes=VMEM_LIMIT, **extra)


def forward_kernel(scal, proj, qkv_out, probs_out, ctx_out, wide):
    heads, tokens, three = qkv_out.shape[1:]
    hd = three // 3
    factor = hd ** (-0.5)
    live = pl.program_id(0) < scal[0]
    qkv = jnp.swapaxes(proj[0], 0, 1)
    qkv_out[0] = qkv
    q, k, v = (qkv[:, :, n * hd : (n + 1) * hd] for n in range(3))
    scores = [lax.dot_general(k[h], q[h], NT, preferred_element_type=F32) for h in range(heads)]
    scores = jnp.stack(scores) * factor
    shifted = jnp.exp(scores - jnp.max(scores, axis=1, keepdims=True))
    probs = shifted * (1.0 / jnp.sum(shifted, axis=1, keepdims=True))
    probs_out[0] = probs
    low = probs.astype(BF16)
    context = [lax.dot_general(v[h], low[h], TN, preferred_element_type=F32) for h in range(heads)]
    for h in range(heads):
        wide[h] = jnp.where(live, context[h], 0.0)
    slots = scal.shape[0] - 2
    for j in range(slots):
        row = pl.multiple_of(scal[2 + j] * 8, 8)
        rows = jnp.concatenate([wide[h, pl.ds(row, 8), :] for h in range(heads)], axis=0)
        ctx_out[j * 8 * heads : (j + 1) * 8 * heads, :] = rows.astype(BF16)


def forward(scal, projections):
    tiles, tokens, heads, three = projections.shape
    hd = three // 3
    return pl.pallas_call(
        forward_kernel,
        grid_spec=pltpu.PrefetchScalarGridSpec(
            num_scalar_prefetch=1,
            grid=(tiles,),
            in_specs=[pl.BlockSpec((1, tokens, heads, three), lambda t, s: (t, 0, 0, 0))],
            out_specs=[
                pl.BlockSpec((1, heads, tokens, three), lambda t, s: (t, 0, 0, 0)),
                pl.BlockSpec((1, heads, tokens, tokens), lambda t, s: (t, 0, 0, 0)),
                pl.BlockSpec((heads * hd, tokens), lambda t, s: (0, t)),
            ],
            scratch_shapes=[pltpu.VMEM((heads, hd, tokens), F32)],
        ),
        out_shape=[
            jax.ShapeDtypeStruct((tiles, heads, tokens, three), BF16),
            jax.ShapeDtypeStruct((tiles, heads, tokens, tokens), F32),
            jax.ShapeDtypeStruct((heads * hd, tiles * tokens), BF16),
        ],
        compiler_params=params(),
        cost_estimate=pl.CostEstimate(
            flops=4 * tiles * heads * tokens * tokens * hd * 4, bytes_accessed=12_000_000, transcendentals=0
        ),
        name="forward",
    )(scal, projections)


def gather_copies(me, pieces, gathered, sem):
    own, plus1, plus2_low, plus2_high, minus1 = pieces
    low = plus2_low.shape[0]

    def copy(n, src, step, tiles=slice(None)):
        return pltpu.make_async_copy(src, gathered.at[tiles, lax.rem(me + step, 4)], sem(n))

    return [
        copy(0, own, 0),
        copy(1, plus1, 1),
        copy(2, plus2_low, 2, pl.ds(0, low)),
        copy(3, plus2_high, 2, pl.ds(low, plus2_high.shape[0])),
        copy(4, minus1, 3),
    ]


def sums_kernel(scal, own, plus1, plus2_low, plus2_high, minus1, ctx, keep, send, gathered, ctx_part, sums, sems):
    tiles, _, tokens, cols = gathered.shape
    loads = [pltpu.make_async_copy(ctx, ctx_part, sems.at[5])]
    loads += gather_copies(scal[1], (own, plus1, plus2_low, plus2_high, minus1), gathered, lambda n: sems.at[n])
    for c in loads:
        c.start()
    for c in loads:
        c.wait()
    step = 2 * LANES
    half = keep.shape[0]
    stores = []
    for low in range(0, cols, step):
        high = min(low + step, cols)
        cot = gathered[:, :, :, low:high].reshape(tiles * 4 * tokens, high - low)
        part = jnp.dot(ctx_part[...], cot, preferred_element_type=F32)
        sums[:, :, low:high] = part.astype(BF16).reshape(sums.shape[0], sums.shape[1], high - low)
    stores = [
        pltpu.make_async_copy(sums.at[half:], send, sems.at[6]),
        pltpu.make_async_copy(sums.at[:half], keep, sems.at[7]),
    ]
    for c in stores:
        c.start()
    for c in stores:
        c.wait()


def weight_sums(scal, pieces, ctx):
    tiles, tokens, cols = pieces[0].shape
    rows, depth = ctx.shape
    any_spec = pl.BlockSpec(memory_space=pl.ANY)
    return pl.pallas_call(
        sums_kernel,
        in_specs=[pl.BlockSpec(memory_space=pltpu.SMEM)] + [any_spec] * 6,
        out_specs=[any_spec] * 2,
        out_shape=[jax.ShapeDtypeStruct((8, rows // 16, cols), BF16)] * 2,
        scratch_shapes=[
            pltpu.VMEM((tiles, 4, tokens, cols), BF16),
            pltpu.VMEM((rows, depth), BF16),
            pltpu.VMEM((16, rows // 16, cols), BF16),
            pltpu.SemaphoreType.DMA((8,)),
        ],
        compiler_params=params(),
        cost_estimate=pl.CostEstimate(flops=8_000_000_000, bytes_accessed=1000, transcendentals=0),
        name="weight_sums",
    )(scal, *pieces, ctx)


def ctx_grad_kernel(groups, cuts, scal, weight, *rest):
    pieces, rest = rest[: 5 * groups], rest[5 * groups :]
    out, gathered, (w, acc, low_acc, sems) = rest[0], rest[1 : 1 + groups], rest[1 + groups :]
    loads = []
    for g, (start, stop) in enumerate(cuts):
        sem = lambda n, g=g: sems.at[6 * g + n]
        cols = pltpu.make_async_copy(weight.at[:, start:stop], w.at[:, start:stop], sem(5))
        loads.append(gather_copies(scal[1], pieces[5 * g : 5 * g + 5], gathered[g], sem) + [cols])
        for c in loads[-1]:
            c.start()
    tiles, blocks, tokens, _ = gathered[0].shape
    rows = tiles * blocks * tokens
    step = rows // 3
    for g, (start, stop) in enumerate(cuts):
        for c in loads[g]:
            c.wait()
        for n in range(3):
            cot = gathered[g][n * (tiles // 3) : (n + 1) * (tiles // 3)].reshape(step, stop - start)
            part = lax.dot_general(cot, w[:, start:stop], NT, preferred_element_type=F32)
            at = slice(n * step, (n + 1) * step)
            part = part if g == 0 else acc[at, :] + part
            if g < groups - 1:
                acc[at, :] = part
            else:
                low_acc[at, :] = part.astype(BF16)
    store = pltpu.make_async_copy(low_acc, out, sems.at[6 * groups])
    store.start()
    store.wait()


def context_gradient(scal, weight, pieces, cuts):
    groups = len(cuts)
    tiles, tokens, _ = pieces[0][0].shape
    rows, width = weight.shape
    depth = tiles * 4 * tokens
    any_spec = pl.BlockSpec(memory_space=pl.ANY)
    return pl.pallas_call(
        functools.partial(ctx_grad_kernel, groups, cuts),
        in_specs=[pl.BlockSpec(memory_space=pltpu.SMEM)] + [any_spec] * (1 + 5 * groups),
        out_specs=any_spec,
        out_shape=jax.ShapeDtypeStruct((depth, rows), BF16),
        scratch_shapes=[pltpu.VMEM((tiles, 4, tokens, stop - start), BF16) for start, stop in cuts]
        + [
            pltpu.VMEM((rows, width), BF16),
            pltpu.VMEM((depth, rows), F32),
            pltpu.VMEM((depth, rows), BF16),
            pltpu.SemaphoreType.DMA((6 * groups + 1,)),
        ],
        compiler_params=params(),
        cost_estimate=pl.CostEstimate(flops=8_000_000_000, bytes_accessed=1000, transcendentals=0),
        name="context_gradient",
    )(scal, weight, *[p for some in pieces for p in some])


def backward_kernel(scal, ctx_grad, qkv, probs, out, ctx_grad_v, qkv_v, probs_v, out_v, grads, sems):
    tiles, heads, tokens, three = qkv_v.shape
    hd = three // 3
    factor = hd ** (-0.5)

    def loads(t):
        rows = pl.ds(pl.multiple_of(t * tokens, tokens), tokens)
        return [
            pltpu.make_async_copy(ctx_grad.at[rows], ctx_grad_v.at[rows], sems.at[0, t]),
            pltpu.make_async_copy(qkv.at[t], qkv_v.at[t], sems.at[1, t]),
            pltpu.make_async_copy(probs.at[t], probs_v.at[t], sems.at[2, t]),
        ]

    def store(t):
        return pltpu.make_async_copy(out_v.at[t], out.at[t], sems.at[3, t])

    for t in range(tiles):
        for c in loads(t):
            c.start()

    def one_tile(t, carry):
        for c in loads(t):
            c.wait()

        @pl.when(t < scal[0])
        def _():
            rows = pl.ds(pl.multiple_of(t * tokens, tokens), tokens)
            q, k, v = (qkv_v[t, :, :, n * hd : (n + 1) * hd] for n in range(3))
            dctx = [ctx_grad_v[rows, h * hd : (h + 1) * hd] for h in range(heads)]
            probs_wide = probs_v[t]
            low = probs_wide.astype(BF16)
            prob_grad = [lax.dot_general(v[h], dctx[h], NT, preferred_element_type=F32) for h in range(heads)]
            value_grad = [jnp.dot(low[h], dctx[h], preferred_element_type=F32) for h in range(heads)]
            prob_grad = jnp.stack(prob_grad)
            centre = jnp.sum(probs_wide * prob_grad, axis=1, keepdims=True)
            score_grad = (probs_wide * (prob_grad - centre) * factor).astype(BF16)
            key_grad = [jnp.dot(score_grad[h], q[h], preferred_element_type=F32) for h in range(heads)]
            query_grad = [
                lax.dot_general(score_grad[h], k[h], TN, preferred_element_type=F32) for h in range(heads)
            ]
            for h in range(heads):
                grads[h, :, 0:hd] = query_grad[h].astype(BF16)
                grads[h, :, hd : 2 * hd] = key_grad[h].astype(BF16)
                grads[h, :, 2 * hd : 3 * hd] = value_grad[h].astype(BF16)
            out_v[t] = jnp.swapaxes(grads[...], 0, 1)

        @pl.when(t >= scal[0])
        def _():
            out_v[t] = jnp.zeros(out_v.shape[1:], BF16)

        store(t).start()
        return carry

    lax.fori_loop(0, tiles, one_tile, 0)
    for t in range(tiles):
        store(t).wait()


def backward(scal, ctx_grad, qkv, probs):
    tiles, heads, tokens, three = qkv.shape
    any_spec = pl.BlockSpec(memory_space=pl.ANY)
    return pl.pallas_call(
        backward_kernel,
        in_specs=[pl.BlockSpec(memory_space=pltpu.SMEM)] + [any_spec] * 3,
        out_specs=any_spec,
        out_shape=jax.ShapeDtypeStruct((tiles, tokens, heads, three), BF16),
        scratch_shapes=[
            pltpu.VMEM(ctx_grad.shape, BF16),
            pltpu.VMEM(qkv.shape, BF16),
            pltpu.VMEM(probs.shape, F32),
            pltpu.VMEM((tiles, tokens, heads, three), BF16),
            pltpu.VMEM((heads, tokens, three), BF16),
            pltpu.SemaphoreType.DMA((4, tiles)),
        ],
        compiler_params=params(),
        cost_estimate=pl.CostEstimate(flops=8_000_000_000, bytes_accessed=1000, transcendentals=0),
        name="backward",
    )(scal, ctx_grad, qkv, probs)


def body(cuts, projections, cotangent, out_weight, tile_counts, fragment, drift):
    dp_size = lax.axis_size("dp")
    fsdp_size = lax.axis_size("fsdp")
    rep_size = lax.axis_size("rep")
    heads, hd, width = out_weight.shape
    me = lax.axis_index("dp")
    core = me % 2

    def flip_core():
        return [(i, i ^ 1) for i in range(dp_size)]

    def shift_x(s):
        return [(i, (i + s) % fsdp_size) for i in range(fsdp_size)]

    slots = [2 * k + (core ^ dc) for dc in range(2) for k in range(dp_size // 2)]
    same_core = [list(range(c, dp_size, 2)) for c in range(2)]
    scal = jnp.stack([tile_counts[0, me], lax.axis_index("fsdp"), *slots]).astype(jnp.int32)

    weight = out_weight.reshape(heads * hd, width)
    n = len(cuts)
    tiles = projections.shape[0]
    st = dict(cot=cotangent)

    def fence(*names):
        flat, tree = jax.tree.flatten({name: st[name] for name in names})
        st.update(jax.tree.unflatten(tree, lax.optimization_barrier(flat)))

    def send_own(i):
        start, stop = cuts[i]
        st[f"own{i}"] = st["cot"][:, :, start:stop]
        st[f"near{i}"] = (
            lax.ppermute(st[f"own{i}"], "fsdp", shift_x(-1)),
            lax.ppermute(st[f"own{i}"], "fsdp", shift_x(1)),
        )

    def pass_on(i):
        split = (tiles + i % 2) // 2
        plus1, minus1 = st[f"near{i}"]
        st[f"far{i}"] = (
            lax.ppermute(plus1[:split], "fsdp", shift_x(-1)),
            lax.ppermute(minus1[split:], "fsdp", shift_x(1)),
        )

    def pieces(i):
        plus1, minus1 = st[f"near{i}"]
        return (st[f"own{i}"], plus1, *st[f"far{i}"], minus1)

    def sum_chunk(i):
        st[f"keep{i}"], st[f"send{i}"] = weight_sums(scal, pieces(i), st["ctx"])

    def cross_core(i):
        st[f"core{i}"] = lax.ppermute(st[f"send{i}"], "dp", flip_core())

    def cross_chips(*some):
        both = [(st[f"keep{i}"].astype(F32) + st[f"core{i}"].astype(F32)).astype(BF16) for i in some]
        both = jnp.concatenate(both, axis=2)
        return lax.all_to_all(both, "dp", 0, 0, axis_index_groups=same_core, tiled=True)

    send_own(0)
    send_own(1)
    qkv, probs, st["ctx"] = forward(scal, projections)
    frag_width = width // FRAGS
    picked = lax.dynamic_slice_in_dim(drift[0], fragment[0] * frag_width, frag_width, 2).astype(BF16)
    every = jnp.broadcast_to(picked[None], (rep_size, *picked.shape))
    st["drift"] = lax.all_to_all(every, "rep", 0, 0, tiled=True)
    fence("ctx", "drift", "near0", "cot")
    pass_on(0)
    send_own(2)
    fence("ctx", "near1", "far0")
    pass_on(1)
    sum_chunk(0)
    fence("ctx", "near2", "far1", "keep0", "send0")
    pass_on(2)
    cross_core(0)
    sum_chunk(1)
    fence("ctx", "far2", "keep0", "core0", "keep1", "send1")
    cross_core(1)
    sum_chunk(2)
    fence("keep0", "core0", "keep1", "core1", "keep2", "send2", "far2")
    cross_core(2)
    summed = cross_chips(0, 1, 2)
    ctx_grad = context_gradient(scal, weight, [pieces(i) for i in range(n)], cuts)
    gradients = backward(scal, ctx_grad, qkv, probs)
    weight_grad = jnp.sum(summed.astype(F32), axis=0) / (CAP * dp_size)
    synced = jnp.sum(st["drift"].astype(F32), axis=0) / rep_size
    return gradients, weight_grad.reshape(drift.shape), synced


def solution(mesh):
    sizes = [9, 10, 6]
    edges = [0]
    for size in sizes:
        edges.append(edges[-1] + size * LANES)
    cuts = list(zip(edges[:-1], edges[1:]))
    return jax.shard_map(
        functools.partial(body, cuts),
        mesh=mesh,
        in_specs=(
            P(("rep", "dp"), None, "fsdp", None),
            P(("rep", "dp"), "fsdp", None),
            P("fsdp", None, None),
            P("rep", None),
            P(),
            P("rep", "fsdp", "dp", None),
        ),
        out_specs=(
            P(("rep", "dp"), None, "fsdp", None),
            P("rep", "fsdp", "dp", None),
            P("fsdp", "dp", None),
        ),
        check_vma=False,
    )
```

time: 446 us -> 109 us (0.24)
  waiting for transfers between devices: 176 us -> 16.8 us
  blocking collectives: 95.7 us -> 0 us
  local copies, waits for them, and re-layouts: 67.3 us -> 8.64 us
  Pallas kernels: 0 us -> 42.1 us
  other arithmetic: 32.6 us -> 3.36 us
  matrix products: 27.5 us -> 0 us
  between operations: 15.6 us -> 1.67 us
  starting transfers between devices: 30.1 us -> 36.1 us
    all_to_all x3 -> x2, waiting for transfers between devices: 100 us -> 4.1 us  [the longest x1 4.09 us: cross_chips(): lax.all_to_all(both, 'dp', 0, 0, axis_index_groups=same_core, tiled=True)]
    psum x1 -> x0, blocking collectives: 95.7 us -> none  [body(): lax.psum(picked.astype(jnp.bfloat16), 'rep').astype(jnp.float32)]
    unnamed x3 -> x0, waiting for transfers between devices: 76.3 us -> none
    pallas_call x0 -> x6, Pallas kernels: none -> 42.1 us  [the longest x3 16.1 us: weight_sums(): pl.pallas_call(sums_kernel, in_specs=[pl.BlockSpec(memory_space=pltpu.SME...]
    gather x9 -> x0, local copies, waits for them, and re-layouts: 40.4 us -> none  [the longest x2 18.1 us: body(): out_proj = jnp.take(projections, send_index, axis=0)]
    dot_general x6 -> x0, matrix products: 25.4 us -> none  [the longest x1 5.91 us: body(): jnp.einsum('sihe,sid->ehd', context, work_dy, preferred_element_type=jnp....]
    ppermute x0 -> x15, starting transfers between devices: none -> 22 us  [the longest x3 7.27 us: pass_on(): lax.ppermute(plus1[:split], 'fsdp', shift_x(-1))]
    select_n x9 -> x0, other arithmetic: 20.6 us -> none  [the longest x2 6.81 us: body(): out_proj = jnp.take(projections, send_index, axis=0)]
  transfers between devices with their start and end apart: 5 -> 17, of which waited for: 3 -> 6; matrix products, arithmetic and copies ran while one was open for 15% -> 7% of each run, Pallas kernels for 0% -> 39%
where the time goes in v1:
time: 109 us
  Pallas kernels  42.1 us (39%)
  starting transfers between devices  36.1 us (33%)
  waiting for transfers between devices  16.8 us (15%)
  local copies, waits for them, and re-layouts  8.64 us (8%)
  other arithmetic  3.36 us (3%)
  between operations  1.67 us (2%)
    pallas_call x3, Pallas kernels, weight_sums(): pl.pallas_call(sums_kernel, in_specs=[pl.BlockSpec(memory_space=pltpu.SME...  16.1 us
    pallas_call x1, Pallas kernels, forward(): pl.pallas_call(forward_kernel, grid_spec=pltpu.PrefetchScalarGridSpec(num...  9.48 us
    pallas_call x1, Pallas kernels, context_gradient(): pl.pallas_call(functools.partial(ctx_grad_kernel, groups, cuts), in_specs...  8.41 us
    all_to_all x1, starting transfers between devices, body(): st['drift'] = lax.all_to_all(every, 'rep', 0, 0, tiled=True)  8.29 us
    pallas_call x1, Pallas kernels, backward(): pl.pallas_call(backward_kernel, in_specs=[pl.BlockSpec(memory_space=pltpu...  8.08 us
    ppermute x3, waiting for transfers between devices, pass_on(): lax.ppermute(minus1[split:], 'fsdp', shift_x(1))  7.88 us
    ppermute x3, starting transfers between devices, pass_on(): lax.ppermute(plus1[:split], 'fsdp', shift_x(-1))  7.27 us
    ppermute x3, starting transfers between devices, send_own(): lax.ppermute(st[f'own{i}'], 'fsdp', shift_x(-1))  6.58 us
  transfers between devices with their start and end apart: 17, of which 6 were waited for; matrix products, arithmetic and copies ran while one was open for 7% of the time, Pallas kernels for 39%

profile of v1, /device:TPU:1, one launch (start us, length us, event | category | flops | bytes accessed | tf_op | source)
XLA Modules:
  0.0 108.6 jit_solution(5394270638109572032)
XLA Ops:
  0.7 1.2 %slice.27.own.rest_0_ = bf16[9,32,1152]{2,1,0:T(8,128)(2,1)S(1)} slice(bf16[9,32,3200]{2,1,0:T(8,128)(2,1)} %param.7), slice={[0:9], [0:32], [0:1152]} | slice | bytes 1327104 | tf_op jit(solution)/shard_map/slice | solution.py:308
  1.9 2.1 %collective-permute-start.1 = (bf16[9,32,1152]{2,1,0:T(8,128)(2,1)S(1)}, bf16[9,32,1152]{2,1,0:T(8,128)(2,1)S(1)}, u32[]{:S(2)}, u32[]{:S(2)}) collective-permute-start(bf16[9,32,1152]{2,1,0:T(8,128)(2,1)S(1)} %slice.27.own.rest_0_), channel_id=1, source_target_pairs={{0,1},{1,2},{2,3},{3,0},{4,5},{5,6},{6,7},{7,4},{8,9},{9,10},{10,1... | collective-permute-start | bytes 1990664 | tf_op jit(solution)/shard_map/ppermute | solution.py:311
  4.0 1.4 %collective-permute-start = (bf16[9,32,1152]{2,1,0:T(8,128)(2,1)S(1)}, bf16[9,32,1152]{2,1,0:T(8,128)(2,1)}, u32[]{:S(2)}, u32[]{:S(2)}) collective-permute-start(bf16[9,32,1152]{2,1,0:T(8,128)(2,1)S(1)} %slice.27.own.rest_0_), channel_id=1, source_target_pairs={{0,3},{1,0},{2,1},{3,2},{4,7},{5,4},{6,5},{7,6},{8,11},{9,8},{10,9... | collective-permute-start | bytes 1990664 | tf_op jit(solution)/shard_map/ppermute | solution.py:310
  5.3 1.2 %slice.30.own.rest_5_ = bf16[9,32,1280]{2,1,0:T(8,128)(2,1)S(1)} slice(bf16[9,32,3200]{2,1,0:T(8,128)(2,1)} %param.7), slice={[0:9], [0:32], [1152:2432]} | slice | bytes 1474560 | tf_op jit(solution)/shard_map/slice | solution.py:308
  6.7 2.6 %collective-permute-start.4 = (bf16[9,32,1280]{2,1,0:T(8,128)(2,1)S(1)}, bf16[9,32,1280]{2,1,0:T(8,128)(2,1)S(1)}, u32[]{:S(2)}, u32[]{:S(2)}) collective-permute-start(bf16[9,32,1280]{2,1,0:T(8,128)(2,1)S(1)} %slice.30.own.rest_5_), channel_id=1, source_target_pairs={{0,3},{1,0},{2,1},{3,2},{4,7},{5,4},{6,5},{7,6},{8,11},{9,8},{10,9... | collective-permute-start | bytes 2211848 | tf_op jit(solution)/shard_map/ppermute | solution.py:310
  10.6 8.3 %all-to-all-start = ((bf16[4,4,8,640]{3,2,1,0:T(8,128)(2,1)}), bf16[4,4,8,640]{3,2,1,0:T(8,128)(2,1)S(1)}, u32[]{:S(2)}, u32[]{:S(2)}) async-start(bf16[4,4,8,640]{3,2,1,0:T(8,128)(2,1)} %broadcast_in_dim.9), calls=%async_computation | async-start | bytes 327680 | tf_op jit(solution)/shard_map/all_to_all | solution.py:343
  19.5 1.3 %stack.71.scal = s32[18]{0:T(128)} concatenate(s32[1]{0:T(128)} %bitcast, s32[1]{0:T(128)} %bitcast.1, s32[1]{0:T(128)} %bitcast.2, s32[1]{0:T(128)} %bitcast.3, s32[1]{0:T(128)} %bitcast.4, s32[1]{0:T(128)} %bitcast.5, s32[1]{0:T(128)} %bitcast.6, s32[1]{0:T(128)} %bitcast.7, s32[1]{0:T(128)} %bitcast.8, s32[1]{0:T(128)} %bitcast.9, s32[1]{0:T(128)} %bitcast.10, s32[1]{0:T(128)} %bitcast.11, ...), dimensions={0} | concatenate | bytes 144 | tf_op jit(solution)/shard_map/stack | solution.py:295
  20.8 9.5 %forward.1 = (bf16[9,4,128,384]{3,2,1,0:T(8,128)(2,1)}, f32[9,4,128,128]{3,2,1,0:T(8,128)}, bf16[512,1152]{1,0:T(8,128)(2,1)}) custom-call(s32[18]{0:T(128)} %stack.71.scal, bf16[9,128,4,384]{3,2,1,0:T(4,128)(2,1)} %proj.1), custom_call_target="tpu_custom_call" | custom-call | flops 1207959552 | bytes 12000000 | tf_op jit(solution)/shard_map/forward/pallas_call | solution.py:56
  30.5 1.1 %slice.28 = bf16[4,32,1152]{2,1,0:T(8,128)(2,1)S(1)} slice(bf16[9,32,1152]{2,1,0:T(8,128)(2,1)} %collective-permute-done.plus1.rest_1_), slice={[0:4], [0:32], [0:1152]} | slice | bytes 589824 | tf_op jit(solution)/shard_map/slice | solution.py:318
  31.6 2.6 %collective-permute-start.2 = (bf16[4,32,1152]{2,1,0:T(8,128)(2,1)S(1)}, bf16[4,32,1152]{2,1,0:T(8,128)(2,1)S(1)}, u32[]{:S(2)}, u32[]{:S(2)}) collective-permute-start(bf16[4,32,1152]{2,1,0:T(8,128)(2,1)S(1)} %slice.28), channel_id=1, source_target_pairs={{0,3},{1,0},{2,1},{3,2},{4,7},{5,4},{6,5},{7,6},{8,11},{9,8},{10,9... | collective-permute-start | bytes 884744 | tf_op jit(solution)/shard_map/ppermute | solution.py:318
  34.2 1.0 slice.33.own.rest_10_
  35.4 2.7 %collective-permute-start.8 = (bf16[9,32,768]{2,1,0:T(8,128)(2,1)S(1)}, bf16[9,32,768]{2,1,0:T(8,128)(2,1)S(1)}, u32[]{:S(2)}, u32[]{:S(2)}) collective-permute-start(bf16[9,32,768]{2,1,0:T(8,128)(2,1)S(1)} %slice.33.own.rest_10_), channel_id=1, source_target_pairs={{0,3},{1,0},{2,1},{3,2},{4,7},{5,4},{6,5},{7,6},{8,11},{9,8},{10,9... | collective-permute-start | bytes 1327112 | tf_op jit(solution)/shard_map/ppermute | solution.py:310
  38.1 3.1 %collective-permute-done.2.plus2_low.rest_2_ = bf16[4,32,1152]{2,1,0:T(8,128)(2,1)S(1)} collective-permute-done((bf16[4,32,1152]{2,1,0:T(8,128)(2,1)S(1)}, bf16[4,32,1152]{2,1,0:T(8,128)(2,1)S(1)}, u32[]{:S(2)}, u32[]{:S(2)}) %collective-permute-start.2) | collective-permute-done | bytes 294944 | tf_op jit(solution)/shard_map/ppermute | solution.py:318
  41.2 1.2 %collective-permute-done.3.plus2_high.rest_3_ = bf16[5,32,1152]{2,1,0:T(8,128)(2,1)S(1)} collective-permute-done((bf16[5,32,1152]{2,1,0:T(8,128)(2,1)S(1)}, bf16[5,32,1152]{2,1,0:T(8,128)(2,1)S(1)}, u32[]{:S(2)}, u32[]{:S(2)}) %collective-permute-start.3) | collective-permute-done | bytes 368672 | tf_op jit(solution)/shard_map/ppermute | solution.py:319
  42.4 1.1 %slice.32 = bf16[4,32,1280]{2,1,0:T(8,128)(2,1)S(1)} slice(bf16[9,32,1280]{2,1,0:T(8,128)(2,1)} %collective-permute-done.5.minus1.rest_9_), slice={[5:9], [0:32], [0:1280]} | slice | bytes 655360 | tf_op jit(solution)/shard_map/slice | solution.py:319
  43.5 0.9 collective-permute-start.7
  44.4 2.0 %collective-permute-start.6 = (bf16[5,32,1280]{2,1,0:T(8,128)(2,1)S(1)}, bf16[5,32,1280]{2,1,0:T(8,128)(2,1)S(1)}, u32[]{:S(2)}, u32[]{:S(2)}) collective-permute-start(bf16[5,32,1280]{2,1,0:T(8,128)(2,1)S(1)} %slice.31), channel_id=1, source_target_pairs={{0,3},{1,0},{2,1},{3,2},{4,7},{5,4},{6,5},{7,6},{8,11},{9,8},{10,9... | collective-permute-start | bytes 1228808 | tf_op jit(solution)/shard_map/ppermute | solution.py:318
  46.4 5.7 %weight_sums.3 = (bf16[8,32,1152]{2,1,0:T(8,128)(2,1)}, bf16[8,32,1152]{2,1,0:T(8,128)(2,1)}) custom-call(s32[18]{0:T(128)} %stack.71.scal, bf16[9,32,1152]{2,1,0:T(8,128)(2,1)} %copy-done.2, bf16[9,32,1152]{2,1,0:T(8,128)(2,1)} %collective-permute-done.plus1.rest_1_, bf16[4,32,1152]{2,1,0:T(8,128)(2,1)} %copy-done.16, bf16[5,32,1152]{2,1,0:T(8,128)(2,1)} %copy-done.14, ...), custom_call_target="tpu_custom_call" | custom-call | flops 8000000000 | bytes 1000 | tf_op jit(solution)/shard_map/weight_sums/pallas_call | solution.py:128
  52.2 6.7 %collective-permute-done.7.plus2_high.rest_8_ = bf16[4,32,1280]{2,1,0:T(8,128)(2,1)S(1)} collective-permute-done((bf16[4,32,1280]{2,1,0:T(8,128)(2,1)S(1)}, bf16[4,32,1280]{2,1,0:T(8,128)(2,1)S(1)}, u32[]{:S(2)}, u32[]{:S(2)}) %collective-permute-start.7) | collective-permute-done | bytes 327712 | tf_op jit(solution)/shard_map/ppermute | solution.py:319
  59.5 2.7 %collective-permute-start.11 = (bf16[4,32,768]{2,1,0:T(8,128)(2,1)S(1)}, bf16[4,32,768]{2,1,0:T(8,128)(2,1)S(1)}, u32[]{:S(2)}, u32[]{:S(2)}) collective-permute-start(bf16[4,32,768]{2,1,0:T(8,128)(2,1)S(1)} %slice.34), channel_id=1, source_target_pairs={{0,3},{1,0},{2,1},{3,2},{4,7},{5,4},{6,5},{7,6},{8,11},{9,8},{10,9... | collective-permute-start | bytes 589832 | tf_op jit(solution)/shard_map/ppermute | solution.py:318
  62.3 2.7 %collective-permute-start.10 = (bf16[8,32,1152]{2,1,0:T(8,128)(2,1)}, bf16[8,32,1152]{2,1,0:T(8,128)(2,1)S(1)}, u32[]{:S(2)}, u32[]{:S(2)}) collective-permute-start(bf16[8,32,1152]{2,1,0:T(8,128)(2,1)} %get-tuple-element.59), channel_id=1, source_target_pairs={{0,4},{4,0},{8,12},{12,8},{16,20},{20,16},{24,28},{28,24},{32,36},... | collective-permute-start | bytes 1769480 | tf_op jit(solution)/shard_map/ppermute | solution.py:330
  65.0 5.8 %weight_sums.4 = (bf16[8,32,1280]{2,1,0:T(8,128)(2,1)}, bf16[8,32,1280]{2,1,0:T(8,128)(2,1)}) custom-call(s32[18]{0:T(128)} %stack.71.scal, bf16[9,32,1280]{2,1,0:T(8,128)(2,1)} %copy-done.1, bf16[9,32,1280]{2,1,0:T(8,128)(2,1)} %copy-done.9, bf16[5,32,1280]{2,1,0:T(8,128)(2,1)} %copy-done.13, bf16[4,32,1280]{2,1,0:T(8,128)(2,1)} %copy-done.15, ...), custom_call_target="tpu_custom_call" | custom-call | flops 8000000000 | bytes 1000 | tf_op jit(solution)/shard_map/weight_sums/pallas_call | solution.py:128
  70.9 1.3 %collective-permute-start.13 = (bf16[8,32,1280]{2,1,0:T(8,128)(2,1)}, bf16[8,32,1280]{2,1,0:T(8,128)(2,1)S(1)}, u32[]{:S(2)}, u32[]{:S(2)}) collective-permute-start(bf16[8,32,1280]{2,1,0:T(8,128)(2,1)} %get-tuple-element.66), channel_id=1, source_target_pairs={{0,4},{4,0},{8,12},{12,8},{16,20},{20,16},{24,28},{28,24},{32,36},... | collective-permute-start | bytes 1966088 | tf_op jit(solution)/shard_map/ppermute | solution.py:330
  72.2 4.6 %weight_sums.5 = (bf16[8,32,768]{2,1,0:T(8,128)(2,1)}, bf16[8,32,768]{2,1,0:T(8,128)(2,1)}) custom-call(s32[18]{0:T(128)} %stack.71.scal, bf16[9,32,768]{2,1,0:T(8,128)(2,1)} %copy-done.7, bf16[9,32,768]{2,1,0:T(8,128)(2,1)} %copy-done.12, bf16[4,32,768]{2,1,0:T(8,128)(2,1)} %copy-done.18, bf16[5,32,768]{2,1,0:T(8,128)(2,1)} %copy-done.17, ...), custom_call_target="tpu_custom_call" | custom-call | flops 8000000000 | bytes 1000 | tf_op jit(solution)/shard_map/weight_sums/pallas_call | solution.py:128
  76.9 0.7 collective-permute-start.14
  78.1 1.0 collective-permute-done.14
  79.2 1.3 %pad_maximum_fusion = bf16[8,32,3200]{2,1,0:T(8,128)(2,1)} fusion(bf16[8,32,768]{2,1,0:T(8,128)(2,1)S(1)} %add_convert_fusion.2, bf16[8,32,1280]{2,1,0:T(8,128)(2,1)S(1)} %add_convert_fusion, bf16[8,32,1152]{2,1,0:T(8,128)(2,1)S(1)} %add_convert_fusion.1), kind=kLoop, calls=%fused_computation.1 | loop fusion | flops 4915200 | bytes 3276800 | tf_op jit(solution)/shard_map/concatenate | solution.py:334
  80.5 5.8 %all-to-all-start.1 = ((bf16[8,32,3200]{2,1,0:T(8,128)(2,1)}), bf16[8,32,3200]{2,1,0:T(8,128)(2,1)S(1)}, u32[]{:S(2)}, u32[]{:S(2)}) async-start(bf16[8,32,3200]{2,1,0:T(8,128)(2,1)} %pad_maximum_fusion), calls=%async_computation.1 | async-start | bytes 3276800 | tf_op jit(solution)/shard_map/all_to_all | solution.py:335
  87.0 8.4 %context_gradient.1.ctx_grad = bf16[1152,512]{1,0:T(8,128)(2,1)} custom-call(s32[18]{0:T(128)} %stack.71.scal, bf16[512,3200]{1,0:T(8,128)(2,1)} %bitcast.24, bf16[9,32,1152]{2,1,0:T(8,128)(2,1)} %copy-done.2, bf16[9,32,1152]{2,1,0:T(8,128)(2,1)} %collective-permute-done.plus1.rest_1_, bf16[4,32,1152]{2,1,0:T(8,128)(2,1)} %copy-done.16, ...), custom_call_target="tpu_custom_call" | custom-call | flops 8000000000 | bytes 1000 | tf_op jit(solution)/shard_map/context_gradient/pallas_call | solution.py:181
  95.4 8.1 %backward.1 = bf16[9,128,4,384]{3,2,1,0:T(4,128)(2,1)} custom-call(s32[18]{0:T(128)} %stack.71.scal, bf16[1152,512]{1,0:T(8,128)(2,1)} %context_gradient.1.ctx_grad, bf16[9,4,128,384]{3,2,1,0:T(8,128)(2,1)} %get-tuple-element.76.qkv, f32[9,4,128,128]{3,2,1,0:T(8,128)} %get-tuple-element.77.probs), custom_call_target="tpu_custom_call" | custom-call | flops 8000000000 | bytes 1000 | tf_op jit(solution)/shard_map/backward/pallas_call | solution.py:260
  103.5 4.1 %all-to-all-done.1 = bf16[8,32,3200]{2,1,0:T(8,128)(2,1)S(1)} async-done(((bf16[8,32,3200]{2,1,0:T(8,128)(2,1)}), bf16[8,32,3200]{2,1,0:T(8,128)(2,1)S(1)}, u32[]{:S(2)}, u32[]{:S(2)}) %all-to-all-start.1) | async-done | bytes 1638432 | tf_op jit(solution)/shard_map/all_to_all | solution.py:335
  107.8 0.8 multiply_bitcast_fusion
  (69 shorter events, 4.0 us)
Async XLA Ops:
  0.6 9.3 %copy-start = (f32[1,4,8,3200]{3,2,1,0:T(8,128)S(1)}, f32[1,4,8,3200]{3,2,1,0:T(8,128)}, u32[]{:S(2)}) copy-start(f32[1,4,8,3200]{3,2,1,0:T(8,128)} %param.11) | copy-start | bytes 1228804
  0.6 18.3 %copy-start.19 = (s32[1,16]{1,0:T(1,128)S(1)}, s32[1,16]{1,0:T(1,128)}, u32[]{:S(2)}) copy-start(s32[1,16]{1,0:T(1,128)} %param.9) | copy-start | bytes 196
  1.9 28.5 %copy-start.2 = (bf16[9,32,1152]{2,1,0:T(8,128)(2,1)}, bf16[9,32,1152]{2,1,0:T(8,128)(2,1)S(1)}, u32[]{:S(2)}) copy-start(bf16[9,32,1152]{2,1,0:T(8,128)(2,1)S(1)} %slice.27.own.rest_0_) | copy-start | bytes 1990660
  1.9 28.5 %collective-permute-start.1 = (bf16[9,32,1152]{2,1,0:T(8,128)(2,1)S(1)}, bf16[9,32,1152]{2,1,0:T(8,128)(2,1)S(1)}, u32[]{:S(2)}, u32[]{:S(2)}) collective-permute-start(bf16[9,32,1152]{2,1,0:T(8,128)(2,1)S(1)} %slice.27.own.rest_0_), channel_id=1, source_target_pairs={{0,1},{1,2},{2,3},{3,0},{4,5},{5,6},{6,7},{7,4},{8,9},{9,10},{10,1... | collective-permute-start | bytes 1990664 | tf_op jit(solution)/shard_map/ppermute | solution.py:311
  4.0 26.4 %collective-permute-start = (bf16[9,32,1152]{2,1,0:T(8,128)(2,1)S(1)}, bf16[9,32,1152]{2,1,0:T(8,128)(2,1)}, u32[]{:S(2)}, u32[]{:S(2)}) collective-permute-start(bf16[9,32,1152]{2,1,0:T(8,128)(2,1)S(1)} %slice.27.own.rest_0_), channel_id=1, source_target_pairs={{0,3},{1,0},{2,1},{3,2},{4,7},{5,4},{6,5},{7,6},{8,11},{9,8},{10,9... | collective-permute-start | bytes 1990664 | tf_op jit(solution)/shard_map/ppermute | solution.py:310
  6.5 23.8 %copy-start.1 = (bf16[9,32,1280]{2,1,0:T(8,128)(2,1)}, bf16[9,32,1280]{2,1,0:T(8,128)(2,1)S(1)}, u32[]{:S(2)}) copy-start(bf16[9,32,1280]{2,1,0:T(8,128)(2,1)S(1)} %slice.30.own.rest_5_) | copy-start | bytes 2211844
  6.5 28.9 %collective-permute-start.5 = (bf16[9,32,1280]{2,1,0:T(8,128)(2,1)S(1)}, bf16[9,32,1280]{2,1,0:T(8,128)(2,1)}, u32[]{:S(2)}, u32[]{:S(2)}) collective-permute-start(bf16[9,32,1280]{2,1,0:T(8,128)(2,1)S(1)} %slice.30.own.rest_5_), channel_id=1, source_target_pairs={{0,1},{1,2},{2,3},{3,0},{4,5},{5,6},{6,7},{7,4},{8,9},{9,10},{10,1... | collective-permute-start | bytes 2211848 | tf_op jit(solution)/shard_map/ppermute | solution.py:311
  6.7 31.4 %collective-permute-start.4 = (bf16[9,32,1280]{2,1,0:T(8,128)(2,1)S(1)}, bf16[9,32,1280]{2,1,0:T(8,128)(2,1)S(1)}, u32[]{:S(2)}, u32[]{:S(2)}) collective-permute-start(bf16[9,32,1280]{2,1,0:T(8,128)(2,1)S(1)} %slice.30.own.rest_5_), channel_id=1, source_target_pairs={{0,3},{1,0},{2,1},{3,2},{4,7},{5,4},{6,5},{7,6},{8,11},{9,8},{10,9... | collective-permute-start | bytes 2211848 | tf_op jit(solution)/shard_map/ppermute | solution.py:310
  10.6 19.7 %all-to-all-start = ((bf16[4,4,8,640]{3,2,1,0:T(8,128)(2,1)}), bf16[4,4,8,640]{3,2,1,0:T(8,128)(2,1)S(1)}, u32[]{:S(2)}, u32[]{:S(2)}) async-start(bf16[4,4,8,640]{3,2,1,0:T(8,128)(2,1)} %broadcast_in_dim.9), calls=%async_computation | async-start | bytes 327680 | tf_op jit(solution)/shard_map/all_to_all | solution.py:343
  30.3 14.1 %copy-start.3 = (bf16[4,4,8,640]{3,2,1,0:T(8,128)(2,1)}, bf16[4,4,8,640]{3,2,1,0:T(8,128)(2,1)S(1)}, u32[]{:S(2)}) copy-start(bf16[4,4,8,640]{3,2,1,0:T(8,128)(2,1)S(1)} %all-to-all-done) | copy-start | bytes 491524
  30.4 16.0 %copy-start.10 = (bf16[9,32,1152]{2,1,0:T(8,128)(2,1)}, bf16[9,32,1152]{2,1,0:T(8,128)(2,1)S(1)}, u32[]{:S(2)}) copy-start(bf16[9,32,1152]{2,1,0:T(8,128)(2,1)S(1)} %collective-permute-done.1.minus1.rest_4_) | copy-start | bytes 1990660
  30.4 12.0 %collective-permute-start.3 = (bf16[5,32,1152]{2,1,0:T(8,128)(2,1)S(1)}, bf16[5,32,1152]{2,1,0:T(8,128)(2,1)S(1)}, u32[]{:S(2)}, u32[]{:S(2)}) collective-permute-start(bf16[5,32,1152]{2,1,0:T(8,128)(2,1)S(1)} %slice.29), channel_id=1, source_target_pairs={{0,1},{1,2},{2,3},{3,0},{4,5},{5,6},{6,7},{7,4},{8,9},{9,10},{10,1... | collective-permute-start | bytes 1105928 | tf_op jit(solution)/shard_map/ppermute | solution.py:319
  31.6 9.6 %collective-permute-start.2 = (bf16[4,32,1152]{2,1,0:T(8,128)(2,1)S(1)}, bf16[4,32,1152]{2,1,0:T(8,128)(2,1)S(1)}, u32[]{:S(2)}, u32[]{:S(2)}) collective-permute-start(bf16[4,32,1152]{2,1,0:T(8,128)(2,1)S(1)} %slice.28), channel_id=1, source_target_pairs={{0,3},{1,0},{2,1},{3,2},{4,7},{5,4},{6,5},{7,6},{8,11},{9,8},{10,9... | collective-permute-start | bytes 884744 | tf_op jit(solution)/shard_map/ppermute | solution.py:318
  35.3 16.8 %copy-start.7 = (bf16[9,32,768]{2,1,0:T(8,128)(2,1)}, bf16[9,32,768]{2,1,0:T(8,128)(2,1)S(1)}, u32[]{:S(2)}) copy-start(bf16[9,32,768]{2,1,0:T(8,128)(2,1)S(1)} %slice.33.own.rest_10_) | copy-start | bytes 1327108
  35.3 16.8 %collective-permute-start.9 = (bf16[9,32,768]{2,1,0:T(8,128)(2,1)S(1)}, bf16[9,32,768]{2,1,0:T(8,128)(2,1)S(1)}, u32[]{:S(2)}, u32[]{:S(2)}) collective-permute-start(bf16[9,32,768]{2,1,0:T(8,128)(2,1)S(1)} %slice.33.own.rest_10_), channel_id=1, source_target_pairs={{0,1},{1,2},{2,3},{3,0},{4,5},{5,6},{6,7},{7,4},{8,9},{9,10},{10,1... | collective-permute-start | bytes 1327112 | tf_op jit(solution)/shard_map/ppermute | solution.py:311
  35.4 16.8 %collective-permute-start.8 = (bf16[9,32,768]{2,1,0:T(8,128)(2,1)S(1)}, bf16[9,32,768]{2,1,0:T(8,128)(2,1)S(1)}, u32[]{:S(2)}, u32[]{:S(2)}) collective-permute-start(bf16[9,32,768]{2,1,0:T(8,128)(2,1)S(1)} %slice.33.own.rest_10_), channel_id=1, source_target_pairs={{0,3},{1,0},{2,1},{3,2},{4,7},{5,4},{6,5},{7,6},{8,11},{9,8},{10,9... | collective-permute-start | bytes 1327112 | tf_op jit(solution)/shard_map/ppermute | solution.py:310
  38.1 14.1 %copy-start.9 = (bf16[9,32,1280]{2,1,0:T(8,128)(2,1)}, bf16[9,32,1280]{2,1,0:T(8,128)(2,1)S(1)}, u32[]{:S(2)}) copy-start(bf16[9,32,1280]{2,1,0:T(8,128)(2,1)S(1)} %collective-permute-done.4.plus1.rest_6_) | copy-start | bytes 2211844
  41.2 5.2 %copy-start.16 = (bf16[4,32,1152]{2,1,0:T(8,128)(2,1)}, bf16[4,32,1152]{2,1,0:T(8,128)(2,1)S(1)}, u32[]{:S(2)}) copy-start(bf16[4,32,1152]{2,1,0:T(8,128)(2,1)S(1)} %collective-permute-done.2.plus2_low.rest_2_) | copy-start | bytes 884740
  43.5 15.4 %collective-permute-start.7 = (bf16[4,32,1280]{2,1,0:T(8,128)(2,1)S(1)}, bf16[4,32,1280]{2,1,0:T(8,128)(2,1)S(1)}, u32[]{:S(2)}, u32[]{:S(2)}) collective-permute-start(bf16[4,32,1280]{2,1,0:T(8,128)(2,1)S(1)} %slice.32), channel_id=1, source_target_pairs={{0,1},{1,2},{2,3},{3,0},{4,5},{5,6},{6,7},{7,4},{8,9},{9,10},{10,1... | collective-permute-start | bytes 983048 | tf_op jit(solution)/shard_map/ppermute | solution.py:319
  44.4 15.0 %collective-permute-start.6 = (bf16[5,32,1280]{2,1,0:T(8,128)(2,1)S(1)}, bf16[5,32,1280]{2,1,0:T(8,128)(2,1)S(1)}, u32[]{:S(2)}, u32[]{:S(2)}) collective-permute-start(bf16[5,32,1280]{2,1,0:T(8,128)(2,1)S(1)} %slice.31), channel_id=1, source_target_pairs={{0,3},{1,0},{2,1},{3,2},{4,7},{5,4},{6,5},{7,6},{8,11},{9,8},{10,9... | collective-permute-start | bytes 1228808 | tf_op jit(solution)/shard_map/ppermute | solution.py:318
  52.2 18.7 %copy-start.11 = (bf16[9,32,768]{2,1,0:T(8,128)(2,1)}, bf16[9,32,768]{2,1,0:T(8,128)(2,1)S(1)}, u32[]{:S(2)}) copy-start(bf16[9,32,768]{2,1,0:T(8,128)(2,1)S(1)} %collective-permute-done.9.minus1.rest_14_) | copy-start | bytes 1327108
  52.2 18.7 %copy-start.12 = (bf16[9,32,768]{2,1,0:T(8,128)(2,1)}, bf16[9,32,768]{2,1,0:T(8,128)(2,1)S(1)}, u32[]{:S(2)}) copy-start(bf16[9,32,768]{2,1,0:T(8,128)(2,1)S(1)} %collective-permute-done.8.plus1.rest_11_) | copy-start | bytes 1327108
  58.9 6.1 %copy-start.15 = (bf16[4,32,1280]{2,1,0:T(8,128)(2,1)}, bf16[4,32,1280]{2,1,0:T(8,128)(2,1)S(1)}, u32[]{:S(2)}) copy-start(bf16[4,32,1280]{2,1,0:T(8,128)(2,1)S(1)} %collective-permute-done.7.plus2_high.rest_8_) | copy-start | bytes 983044
  59.5 5.5 %copy-start.13 = (bf16[5,32,1280]{2,1,0:T(8,128)(2,1)}, bf16[5,32,1280]{2,1,0:T(8,128)(2,1)S(1)}, u32[]{:S(2)}) copy-start(bf16[5,32,1280]{2,1,0:T(8,128)(2,1)S(1)} %collective-permute-done.6.plus2_low.rest_7_) | copy-start | bytes 1228804
  59.5 11.4 %collective-permute-start.11 = (bf16[4,32,768]{2,1,0:T(8,128)(2,1)S(1)}, bf16[4,32,768]{2,1,0:T(8,128)(2,1)S(1)}, u32[]{:S(2)}, u32[]{:S(2)}) collective-permute-start(bf16[4,32,768]{2,1,0:T(8,128)(2,1)S(1)} %slice.34), channel_id=1, source_target_pairs={{0,3},{1,0},{2,1},{3,2},{4,7},{5,4},{6,5},{7,6},{8,11},{9,8},{10,9... | collective-permute-start | bytes 589832 | tf_op jit(solution)/shard_map/ppermute | solution.py:318
  62.2 8.7 %collective-permute-start.12 = (bf16[5,32,768]{2,1,0:T(8,128)(2,1)S(1)}, bf16[5,32,768]{2,1,0:T(8,128)(2,1)S(1)}, u32[]{:S(2)}, u32[]{:S(2)}) collective-permute-start(bf16[5,32,768]{2,1,0:T(8,128)(2,1)S(1)} %slice.35), channel_id=1, source_target_pairs={{0,1},{1,2},{2,3},{3,0},{4,5},{5,6},{6,7},{7,4},{8,9},{9,10},{10,1... | collective-permute-start | bytes 737288 | tf_op jit(solution)/shard_map/ppermute | solution.py:319
  62.3 8.6 %collective-permute-start.10 = (bf16[8,32,1152]{2,1,0:T(8,128)(2,1)}, bf16[8,32,1152]{2,1,0:T(8,128)(2,1)S(1)}, u32[]{:S(2)}, u32[]{:S(2)}) collective-permute-start(bf16[8,32,1152]{2,1,0:T(8,128)(2,1)} %get-tuple-element.59), channel_id=1, source_target_pairs={{0,4},{4,0},{8,12},{12,8},{16,20},{20,16},{24,28},{28,24},{32,36},... | collective-permute-start | bytes 1769480 | tf_op jit(solution)/shard_map/ppermute | solution.py:330
  70.9 6.7 %copy-start.6 = (bf16[8,32,1152]{2,1,0:T(8,128)(2,1)S(1)}, bf16[8,32,1152]{2,1,0:T(8,128)(2,1)}, u32[]{:S(2)}) copy-start(bf16[8,32,1152]{2,1,0:T(8,128)(2,1)} %get-tuple-element.78) | copy-start | bytes 1769476
  70.9 6.0 %collective-permute-start.13 = (bf16[8,32,1280]{2,1,0:T(8,128)(2,1)}, bf16[8,32,1280]{2,1,0:T(8,128)(2,1)S(1)}, u32[]{:S(2)}, u32[]{:S(2)}) collective-permute-start(bf16[8,32,1280]{2,1,0:T(8,128)(2,1)} %get-tuple-element.66), channel_id=1, source_target_pairs={{0,4},{4,0},{8,12},{12,8},{16,20},{20,16},{24,28},{28,24},{32,36},... | collective-permute-start | bytes 1966088 | tf_op jit(solution)/shard_map/ppermute | solution.py:330
  76.9 2.3 %collective-permute-start.14 = (bf16[8,32,768]{2,1,0:T(8,128)(2,1)}, bf16[8,32,768]{2,1,0:T(8,128)(2,1)S(1)}, u32[]{:S(2)}, u32[]{:S(2)}) collective-permute-start(bf16[8,32,768]{2,1,0:T(8,128)(2,1)} %get-tuple-element.83), channel_id=1, source_target_pairs={{0,4},{4,0},{8,12},{12,8},{16,20},{20,16},{24,28},{28,24},{32,36},... | collective-permute-start | bytes 1179656 | tf_op jit(solution)/shard_map/ppermute | solution.py:330
  80.5 5.8 %copy-start.4 = (bf16[4,4,8,640]{3,2,1,0:T(8,128)(2,1)S(1)}, bf16[4,4,8,640]{3,2,1,0:T(8,128)(2,1)}, u32[]{:S(2)}) copy-start(bf16[4,4,8,640]{3,2,1,0:T(8,128)(2,1)} %copy-done.3) | copy-start | bytes 491524
  80.5 27.1 %all-to-all-start.1 = ((bf16[8,32,3200]{2,1,0:T(8,128)(2,1)}), bf16[8,32,3200]{2,1,0:T(8,128)(2,1)S(1)}, u32[]{:S(2)}, u32[]{:S(2)}) async-start(bf16[8,32,3200]{2,1,0:T(8,128)(2,1)} %pad_maximum_fusion), calls=%async_computation.1 | async-start | bytes 3276800 | tf_op jit(solution)/shard_map/all_to_all | solution.py:335
  (5 other events, 10.1 us)

commit v2 on v1

--- a/solution.py
+++ b/solution.py
@@ -10,7 +10,7 @@
 CAP = 6
 FRAGS = 5
 LANES = 128
-VMEM_LIMIT = 56 * 1024 * 1024
+LARGE, SMALL = 56 * 1024 * 1024, 20 * 1024 * 1024
 F32 = jnp.float32
 BF16 = jnp.bfloat16
 
@@ -22,8 +22,8 @@
     return pl.BlockSpec(memory_space=pltpu.VMEM)
 
 
-def params(**extra):
-    return pltpu.CompilerParams(vmem_limit_bytes=VMEM_LIMIT, **extra)
+def params(limit):
+    return pltpu.CompilerParams(vmem_limit_bytes=limit)
 
 
 def forward_kernel(scal, proj, qkv_out, probs_out, ctx_out, wide):
@@ -71,7 +71,7 @@
             jax.ShapeDtypeStruct((tiles, heads, tokens, tokens), F32),
             jax.ShapeDtypeStruct((heads * hd, tiles * tokens), BF16),
         ],
-        compiler_params=params(),
+        compiler_params=params(LARGE),
         cost_estimate=pl.CostEstimate(
             flops=4 * tiles * heads * tokens * tokens * hd * 4, bytes_accessed=12_000_000, transcendentals=0
         ),
@@ -95,28 +95,42 @@
     ]
 
 
+def column_parts(cols):
+    middle = (cols // LANES + 1) // 2 * LANES
+    return [(0, middle), (middle, cols)]
+
+
 def sums_kernel(scal, own, plus1, plus2_low, plus2_high, minus1, ctx, keep, send, gathered, ctx_part, sums, sems):
     tiles, _, tokens, cols = gathered.shape
-    loads = [pltpu.make_async_copy(ctx, ctx_part, sems.at[5])]
-    loads += gather_copies(scal[1], (own, plus1, plus2_low, plus2_high, minus1), gathered, lambda n: sems.at[n])
-    for c in loads:
-        c.start()
-    for c in loads:
-        c.wait()
-    step = 2 * LANES
+    parts = column_parts(cols)
     half = keep.shape[0]
+    first = pltpu.make_async_copy(ctx, ctx_part, sems.at[0, 5])
+    first.start()
+    loads = []
+    for n, (low, high) in enumerate(parts):
+        sides = [r.at[:, :, low:high] for r in (own, plus1, plus2_low, plus2_high, minus1)]
+        loads.append(
+            gather_copies(scal[1], sides, gathered.at[:, :, :, low:high], lambda m, n=n: sems.at[n, m])
+        )
+        for c in loads[-1]:
+            c.start()
+    first.wait()
     stores = []
-    for low in range(0, cols, step):
-        high = min(low + step, cols)
+    for n, (low, high) in enumerate(parts):
+        for c in loads[n]:
+            c.wait()
         cot = gathered[:, :, :, low:high].reshape(tiles * 4 * tokens, high - low)
-        part = jnp.dot(ctx_part[...], cot, preferred_element_type=F32)
-        sums[:, :, low:high] = part.astype(BF16).reshape(sums.shape[0], sums.shape[1], high - low)
-    stores = [
-        pltpu.make_async_copy(sums.at[half:], send, sems.at[6]),
-        pltpu.make_async_copy(sums.at[:half], keep, sems.at[7]),
-    ]
-    for c in stores:
-        c.start()
+        for m, (out, at) in enumerate([(send, half), (keep, 0)]):
+            rows = half * sums.shape[1]
+            mine = ctx_part[at * sums.shape[1] : at * sums.shape[1] + rows, :]
+            part = jnp.dot(mine, cot, preferred_element_type=F32)
+            sums[at : at + half, :, low:high] = part.astype(BF16).reshape(half, sums.shape[1], high - low)
+            stores.append(
+                pltpu.make_async_copy(
+                    sums.at[at : at + half, :, low:high], out.at[:, :, low:high], sems.at[n, 6 + m]
+                )
+            )
+            stores[-1].start()
     for c in stores:
         c.wait()
 
@@ -134,9 +148,9 @@
             pltpu.VMEM((tiles, 4, tokens, cols), BF16),
             pltpu.VMEM((rows, depth), BF16),
             pltpu.VMEM((16, rows // 16, cols), BF16),
-            pltpu.SemaphoreType.DMA((8,)),
+            pltpu.SemaphoreType.DMA((2, 8)),
         ],
-        compiler_params=params(),
+        compiler_params=params(SMALL),
         cost_estimate=pl.CostEstimate(flops=8_000_000_000, bytes_accessed=1000, transcendentals=0),
         name="weight_sums",
     )(scal, *pieces, ctx)
@@ -190,7 +204,7 @@
             pltpu.VMEM((depth, rows), BF16),
             pltpu.SemaphoreType.DMA((6 * groups + 1,)),
         ],
-        compiler_params=params(),
+        compiler_params=params(LARGE),
         cost_estimate=pl.CostEstimate(flops=8_000_000_000, bytes_accessed=1000, transcendentals=0),
         name="context_gradient",
     )(scal, weight, *[p for some in pieces for p in some])
@@ -270,7 +284,7 @@
             pltpu.VMEM((heads, tokens, three), BF16),
             pltpu.SemaphoreType.DMA((4, tiles)),
         ],
-        compiler_params=params(),
+        compiler_params=params(LARGE),
         cost_estimate=pl.CostEstimate(flops=8_000_000_000, bytes_accessed=1000, transcendentals=0),
         name="backward",
     )(scal, ctx_grad, qkv, probs)
@@ -347,25 +361,26 @@
     fence("ctx", "near1", "far0")
     pass_on(1)
     sum_chunk(0)
-    fence("ctx", "near2", "far1", "keep0", "send0")
+    fence("near2", "keep0", "send0")
     pass_on(2)
     cross_core(0)
+    fence("ctx", "far1")
     sum_chunk(1)
     fence("ctx", "far2", "keep0", "core0", "keep1", "send1")
     cross_core(1)
     sum_chunk(2)
     fence("keep0", "core0", "keep1", "core1", "keep2", "send2", "far2")
     cross_core(2)
-    summed = cross_chips(0, 1, 2)
+    summed = [cross_chips(0, 1, 2)]
     ctx_grad = context_gradient(scal, weight, [pieces(i) for i in range(n)], cuts)
     gradients = backward(scal, ctx_grad, qkv, probs)
-    weight_grad = jnp.sum(summed.astype(F32), axis=0) / (CAP * dp_size)
+    weight_grad = jnp.concatenate([jnp.sum(p.astype(F32), axis=0) for p in summed], axis=1) / (CAP * dp_size)
     synced = jnp.sum(st["drift"].astype(F32), axis=0) / rep_size
     return gradients, weight_grad.reshape(drift.shape), synced
 
 
 def solution(mesh):
-    sizes = [9, 10, 6]
+    sizes = [8, 10, 7]
     edges = [0]
     for size in sizes:
         edges.append(edges[-1] + size * LANES)

time: 109 us -> 103 us (0.945)
  waiting for transfers between devices: 16.8 us -> 11.4 us
  Pallas kernels: 42.1 us -> 37.2 us
  starting transfers between devices: 36.1 us -> 39.4 us
    ppermute x3, waiting for transfers between devices: 7.88 us -> 0.75 us  [pass_on(): lax.ppermute(minus1[split:], 'fsdp', shift_x(1))]
    pallas_call x3, Pallas kernels: 16.1 us -> 12.3 us  [weight_sums(): pl.pallas_call(sums_kernel, in_specs=[pl.BlockSpec(memory_space=pltpu.SME...]
    ppermute x3, starting transfers between devices: 4.74 us -> 8.6 us  [cross_core(): st[f'core{i}'] = lax.ppermute(st[f'send{i}'], 'dp', flip_core())]
    ppermute x3, waiting for transfers between devices: 0.01 us -> 3.44 us  [send_own(): lax.ppermute(st[f'own{i}'], 'fsdp', shift_x(1))]
    ppermute x3, waiting for transfers between devices: 3.72 us -> 0.68 us  [pass_on(): lax.ppermute(plus1[:split], 'fsdp', shift_x(-1))]
  transfers between devices with their start and end apart: 17 -> 17, of which waited for: 6 -> 5; matrix products, arithmetic and copies ran while one was open for 7% -> 9% of each run, Pallas kernels for 39% -> 36%
where the time goes in v2:
time: 103 us; the launch traced here: 102 us
  starting transfers between devices  39.4 us (38%)
  Pallas kernels  37.2 us (36%)
  waiting for transfers between devices  11.4 us (11%)
  local copies, waits for them, and re-layouts  9.27 us (9%)
  other arithmetic  3.45 us (3%)
  between operations  1.64 us (2%)
    pallas_call x3, Pallas kernels, weight_sums(): pl.pallas_call(sums_kernel, in_specs=[pl.BlockSpec(memory_space=pltpu.SME...  12.3 us
    pallas_call x1, Pallas kernels, forward(): pl.pallas_call(forward_kernel, grid_spec=pltpu.PrefetchScalarGridSpec(num...  9.49 us
    ppermute x3, starting transfers between devices, cross_core(): st[f'core{i}'] = lax.ppermute(st[f'send{i}'], 'dp', flip_core())  8.6 us
    pallas_call x1, Pallas kernels, context_gradient(): pl.pallas_call(functools.partial(ctx_grad_kernel, groups, cuts), in_specs...  8.3 us
    all_to_all x1, starting transfers between devices, body(): st['drift'] = lax.all_to_all(every, 'rep', 0, 0, tiled=True)  8.29 us
    ppermute x3, starting transfers between devices, pass_on(): lax.ppermute(plus1[:split], 'fsdp', shift_x(-1))  7.24 us
    pallas_call x1, Pallas kernels, backward(): pl.pallas_call(backward_kernel, in_specs=[pl.BlockSpec(memory_space=pltpu...  7.18 us
    ppermute x3, starting transfers between devices, send_own(): lax.ppermute(st[f'own{i}'], 'fsdp', shift_x(-1))  6.58 us
  transfers between devices with their start and end apart: 17, of which 5 were waited for; matrix products, arithmetic and copies ran while one was open for 9% of the time, Pallas kernels for 36%

profile of v2, /device:TPU:1, one launch (start us, length us, event | category | flops | bytes accessed | tf_op | source)
XLA Modules:
  0.0 102.4 jit_solution(13921792341910155136)
XLA Ops:
  0.7 1.2 %slice.27.own.rest_0_ = bf16[9,32,1024]{2,1,0:T(8,128)(2,1)S(1)} slice(bf16[9,32,3200]{2,1,0:T(8,128)(2,1)} %param.7), slice={[0:9], [0:32], [0:1024]} | slice | bytes 1179648 | tf_op jit(solution)/shard_map/slice | solution.py:322
  1.8 2.1 %collective-permute-start.1 = (bf16[9,32,1024]{2,1,0:T(8,128)(2,1)S(1)}, bf16[9,32,1024]{2,1,0:T(8,128)(2,1)}, u32[]{:S(2)}, u32[]{:S(2)}) collective-permute-start(bf16[9,32,1024]{2,1,0:T(8,128)(2,1)S(1)} %slice.27.own.rest_0_), channel_id=1, source_target_pairs={{0,1},{1,2},{2,3},{3,0},{4,5},{5,6},{6,7},{7,4},{8,9},{9,10},{10,1... | collective-permute-start | bytes 1769480 | tf_op jit(solution)/shard_map/ppermute | solution.py:325
  4.0 1.4 %collective-permute-start = (bf16[9,32,1024]{2,1,0:T(8,128)(2,1)S(1)}, bf16[9,32,1024]{2,1,0:T(8,128)(2,1)}, u32[]{:S(2)}, u32[]{:S(2)}) collective-permute-start(bf16[9,32,1024]{2,1,0:T(8,128)(2,1)S(1)} %slice.27.own.rest_0_), channel_id=1, source_target_pairs={{0,3},{1,0},{2,1},{3,2},{4,7},{5,4},{6,5},{7,6},{8,11},{9,8},{10,9... | collective-permute-start | bytes 1769480 | tf_op jit(solution)/shard_map/ppermute | solution.py:324
  5.3 1.2 %slice.30.own.rest_5_ = bf16[9,32,1280]{2,1,0:T(8,128)(2,1)S(1)} slice(bf16[9,32,3200]{2,1,0:T(8,128)(2,1)} %param.7), slice={[0:9], [0:32], [1024:2304]} | slice | bytes 1474560 | tf_op jit(solution)/shard_map/slice | solution.py:322
  6.7 2.6 %collective-permute-start.4 = (bf16[9,32,1280]{2,1,0:T(8,128)(2,1)S(1)}, bf16[9,32,1280]{2,1,0:T(8,128)(2,1)S(1)}, u32[]{:S(2)}, u32[]{:S(2)}) collective-permute-start(bf16[9,32,1280]{2,1,0:T(8,128)(2,1)S(1)} %slice.30.own.rest_5_), channel_id=1, source_target_pairs={{0,3},{1,0},{2,1},{3,2},{4,7},{5,4},{6,5},{7,6},{8,11},{9,8},{10,9... | collective-permute-start | bytes 2211848 | tf_op jit(solution)/shard_map/ppermute | solution.py:324
  9.9 0.7 broadcast_in_dim.9
  10.6 8.3 %all-to-all-start = ((bf16[4,4,8,640]{3,2,1,0:T(8,128)(2,1)}), bf16[4,4,8,640]{3,2,1,0:T(8,128)(2,1)S(1)}, u32[]{:S(2)}, u32[]{:S(2)}) async-start(bf16[4,4,8,640]{3,2,1,0:T(8,128)(2,1)} %broadcast_in_dim.9), calls=%async_computation | async-start | bytes 327680 | tf_op jit(solution)/shard_map/all_to_all | solution.py:357
  19.5 1.3 %stack.71.scal = s32[18]{0:T(128)} concatenate(s32[1]{0:T(128)} %bitcast, s32[1]{0:T(128)} %bitcast.1, s32[1]{0:T(128)} %bitcast.2, s32[1]{0:T(128)} %bitcast.3, s32[1]{0:T(128)} %bitcast.4, s32[1]{0:T(128)} %bitcast.5, s32[1]{0:T(128)} %bitcast.6, s32[1]{0:T(128)} %bitcast.7, s32[1]{0:T(128)} %bitcast.8, s32[1]{0:T(128)} %bitcast.9, s32[1]{0:T(128)} %bitcast.10, s32[1]{0:T(128)} %bitcast.11, ...), dimensions={0} | concatenate | bytes 144 | tf_op jit(solution)/shard_map/stack | solution.py:309
  20.7 9.5 %forward.1 = (bf16[9,4,128,384]{3,2,1,0:T(8,128)(2,1)}, f32[9,4,128,128]{3,2,1,0:T(8,128)}, bf16[512,1152]{1,0:T(8,128)(2,1)}) custom-call(s32[18]{0:T(128)} %stack.71.scal, bf16[9,128,4,384]{3,2,1,0:T(4,128)(2,1)} %proj.1), custom_call_target="tpu_custom_call" | custom-call | flops 1207959552 | bytes 12000000 | tf_op jit(solution)/shard_map/forward/pallas_call | solution.py:56
  30.3 1.1 %slice.29 = bf16[5,32,1024]{2,1,0:T(8,128)(2,1)S(1)} slice(bf16[9,32,1024]{2,1,0:T(8,128)(2,1)} %collective-permute-done.1.minus1.rest_4_), slice={[4:9], [0:32], [0:1024]} | slice | bytes 655360 | tf_op jit(solution)/shard_map/slice | solution.py:333
  31.5 1.0 slice.28
  32.4 2.7 %collective-permute-start.2 = (bf16[4,32,1024]{2,1,0:T(8,128)(2,1)S(1)}, bf16[4,32,1024]{2,1,0:T(8,128)(2,1)S(1)}, u32[]{:S(2)}, u32[]{:S(2)}) collective-permute-start(bf16[4,32,1024]{2,1,0:T(8,128)(2,1)S(1)} %slice.28), channel_id=1, source_target_pairs={{0,3},{1,0},{2,1},{3,2},{4,7},{5,4},{6,5},{7,6},{8,11},{9,8},{10,9... | collective-permute-start | bytes 786440 | tf_op jit(solution)/shard_map/ppermute | solution.py:332
  35.2 1.1 %slice.33.own.rest_10_ = bf16[9,32,896]{2,1,0:T(8,128)(2,1)S(1)} slice(bf16[9,32,3200]{2,1,0:T(8,128)(2,1)} %param.7), slice={[0:9], [0:32], [2304:3200]} | slice | bytes 1032192 | tf_op jit(solution)/shard_map/slice | solution.py:322
  36.4 2.7 %collective-permute-start.8 = (bf16[9,32,896]{2,1,0:T(8,128)(2,1)S(1)}, bf16[9,32,896]{2,1,0:T(8,128)(2,1)S(1)}, u32[]{:S(2)}, u32[]{:S(2)}) collective-permute-start(bf16[9,32,896]{2,1,0:T(8,128)(2,1)S(1)} %slice.33.own.rest_10_), channel_id=1, source_target_pairs={{0,3},{1,0},{2,1},{3,2},{4,7},{5,4},{6,5},{7,6},{8,11},{9,8},{10,9... | collective-permute-start | bytes 1548296 | tf_op jit(solution)/shard_map/ppermute | solution.py:324
  39.0 0.7 collective-permute-done.3.plus2_high.rest_3_
  39.8 1.1 %slice.32 = bf16[4,32,1280]{2,1,0:T(8,128)(2,1)S(1)} slice(bf16[9,32,1280]{2,1,0:T(8,128)(2,1)} %collective-permute-done.5.minus1.rest_9_), slice={[5:9], [0:32], [0:1280]} | slice | bytes 655360 | tf_op jit(solution)/shard_map/slice | solution.py:333
  40.9 1.0 collective-permute-start.7
  42.0 1.8 %collective-permute-start.6 = (bf16[5,32,1280]{2,1,0:T(8,128)(2,1)S(1)}, bf16[5,32,1280]{2,1,0:T(8,128)(2,1)S(1)}, u32[]{:S(2)}, u32[]{:S(2)}) collective-permute-start(bf16[5,32,1280]{2,1,0:T(8,128)(2,1)S(1)} %slice.31), channel_id=1, source_target_pairs={{0,3},{1,0},{2,1},{3,2},{4,7},{5,4},{6,5},{7,6},{8,11},{9,8},{10,9... | collective-permute-start | bytes 1228808 | tf_op jit(solution)/shard_map/ppermute | solution.py:332
  43.8 4.1 %weight_sums.3 = (bf16[8,32,1024]{2,1,0:T(8,128)(2,1)S(1)}, bf16[8,32,1024]{2,1,0:T(8,128)(2,1)S(1)}) custom-call(s32[18]{0:T(128)S(1)} %copy-done.7, bf16[9,32,1024]{2,1,0:T(8,128)(2,1)S(1)} %slice.27.own.rest_0_, bf16[9,32,1024]{2,1,0:T(8,128)(2,1)} %collective-permute-done.plus1.rest_1_, ...), custom_call_target="tpu_custom_call" | custom-call | flops 8000000000 | bytes 1000 | tf_op jit(solution)/shard_map/weight_sums/pallas_call | solution.py:142
  48.0 3.4 %collective-permute-done.9.minus1.rest_14_ = bf16[9,32,896]{2,1,0:T(8,128)(2,1)S(1)} collective-permute-done((bf16[9,32,896]{2,1,0:T(8,128)(2,1)S(1)}, bf16[9,32,896]{2,1,0:T(8,128)(2,1)S(1)}, u32[]{:S(2)}, u32[]{:S(2)}) %collective-permute-start.9) | collective-permute-done | bytes 516128 | tf_op jit(solution)/shard_map/ppermute | solution.py:325
  51.4 2.7 %collective-permute-start.11 = (bf16[4,32,896]{2,1,0:T(8,128)(2,1)S(1)}, bf16[4,32,896]{2,1,0:T(8,128)(2,1)S(1)}, u32[]{:S(2)}, u32[]{:S(2)}) collective-permute-start(bf16[4,32,896]{2,1,0:T(8,128)(2,1)S(1)} %slice.34), channel_id=1, source_target_pairs={{0,3},{1,0},{2,1},{3,2},{4,7},{5,4},{6,5},{7,6},{8,11},{9,8},{10,9... | collective-permute-start | bytes 688136 | tf_op jit(solution)/shard_map/ppermute | solution.py:332
  54.2 4.5 %collective-permute-start.10 = (bf16[8,32,1024]{2,1,0:T(8,128)(2,1)S(1)}, bf16[8,32,1024]{2,1,0:T(8,128)(2,1)S(1)}, u32[]{:S(2)}, u32[]{:S(2)}) collective-permute-start(bf16[8,32,1024]{2,1,0:T(8,128)(2,1)S(1)} %get-tuple-element.59), channel_id=1, source_target_pairs={{0,4},{4,0},{8,12},{12,8},{16,20},{20,16},{24,28},{28,24},{32,36},... | collective-permute-start | bytes 1572872 | tf_op jit(solution)/shard_map/ppermute | solution.py:344
  59.4 4.9 %weight_sums.4 = (bf16[8,32,1280]{2,1,0:T(8,128)(2,1)S(1)}, bf16[8,32,1280]{2,1,0:T(8,128)(2,1)S(1)}) custom-call(s32[18]{0:T(128)S(1)} %copy-done.7, bf16[9,32,1280]{2,1,0:T(8,128)(2,1)S(1)} %slice.30.own.rest_5_, bf16[9,32,1280]{2,1,0:T(8,128)(2,1)S(1)} %collective-permute-done.4.plus1.rest_6_, ...), custom_call_target="tpu_custom_call" | custom-call | flops 8000000000 | bytes 1000 | tf_op jit(solution)/shard_map/weight_sums/pallas_call | solution.py:142
  64.3 4.0 %collective-permute-start.13 = (bf16[8,32,1280]{2,1,0:T(8,128)(2,1)S(1)}, bf16[8,32,1280]{2,1,0:T(8,128)(2,1)S(1)}, u32[]{:S(2)}, u32[]{:S(2)}) collective-permute-start(bf16[8,32,1280]{2,1,0:T(8,128)(2,1)S(1)} %get-tuple-element.66), channel_id=1, source_target_pairs={{0,4},{4,0},{8,12},{12,8},{16,20},{20,16},{24,28},{28,24},{32,36},... | collective-permute-start | bytes 1966088 | tf_op jit(solution)/shard_map/ppermute | solution.py:344
  68.4 3.3 %weight_sums.5 = (bf16[8,32,896]{2,1,0:T(8,128)(2,1)S(1)}, bf16[8,32,896]{2,1,0:T(8,128)(2,1)S(1)}) custom-call(s32[18]{0:T(128)S(1)} %copy-done.7, bf16[9,32,896]{2,1,0:T(8,128)(2,1)S(1)} %slice.33.own.rest_10_, bf16[9,32,896]{2,1,0:T(8,128)(2,1)S(1)} %collective-permute-done.8.plus1.rest_11_, ...), custom_call_target="tpu_custom_call" | custom-call | flops 8000000000 | bytes 1000 | tf_op jit(solution)/shard_map/weight_sums/pallas_call | solution.py:142
  72.1 1.4 %collective-permute-done.14 = bf16[8,32,896]{2,1,0:T(8,128)(2,1)S(1)} collective-permute-done((bf16[8,32,896]{2,1,0:T(8,128)(2,1)S(1)}, bf16[8,32,896]{2,1,0:T(8,128)(2,1)S(1)}, u32[]{:S(2)}, u32[]{:S(2)}) %collective-permute-start.14) | collective-permute-done | bytes 458784 | tf_op jit(solution)/shard_map/ppermute | solution.py:344
  73.7 1.3 %pad_maximum_fusion = bf16[8,32,3200]{2,1,0:T(8,128)(2,1)} fusion(bf16[8,32,896]{2,1,0:T(8,128)(2,1)S(1)} %add_convert_fusion.2, bf16[8,32,1280]{2,1,0:T(8,128)(2,1)S(1)} %add_convert_fusion, bf16[8,32,1024]{2,1,0:T(8,128)(2,1)S(1)} %add_convert_fusion.1), kind=kLoop, calls=%fused_computation.1 | loop fusion | flops 4915200 | bytes 3276800 | tf_op jit(solution)/shard_map/concatenate | solution.py:348
  75.0 5.1 %all-to-all-start.1 = ((bf16[8,32,3200]{2,1,0:T(8,128)(2,1)}), bf16[8,32,3200]{2,1,0:T(8,128)(2,1)S(1)}, u32[]{:S(2)}, u32[]{:S(2)}) async-start(bf16[8,32,3200]{2,1,0:T(8,128)(2,1)} %pad_maximum_fusion), calls=%async_computation.1 | async-start | bytes 3276800 | tf_op jit(solution)/shard_map/all_to_all | solution.py:349
  80.8 8.3 %context_gradient.1.ctx_grad = bf16[1152,512]{1,0:T(8,128)(2,1)} custom-call(s32[18]{0:T(128)} %stack.71.scal, bf16[512,3200]{1,0:T(8,128)(2,1)} %bitcast.24, bf16[9,32,1024]{2,1,0:T(8,128)(2,1)} %copy-done.2, bf16[9,32,1024]{2,1,0:T(8,128)(2,1)} %collective-permute-done.plus1.rest_1_, bf16[4,32,1024]{2,1,0:T(8,128)(2,1)} %copy-done.12, ...), custom_call_target="tpu_custom_call" | custom-call | flops 8000000000 | bytes 1000 | tf_op jit(solution)/shard_map/context_gradient/pallas_call | solution.py:195
  89.1 7.2 %backward.1 = bf16[9,128,4,384]{3,2,1,0:T(4,128)(2,1)} custom-call(s32[18]{0:T(128)} %stack.71.scal, bf16[1152,512]{1,0:T(8,128)(2,1)} %context_gradient.1.ctx_grad, bf16[9,4,128,384]{3,2,1,0:T(8,128)(2,1)} %get-tuple-element.76.qkv, f32[9,4,128,128]{3,2,1,0:T(8,128)} %get-tuple-element.77.probs), custom_call_target="tpu_custom_call" | custom-call | flops 8000000000 | bytes 1000 | tf_op jit(solution)/shard_map/backward/pallas_call | solution.py:274
  96.3 5.1 %all-to-all-done.1 = bf16[8,32,3200]{2,1,0:T(8,128)(2,1)S(1)} async-done(((bf16[8,32,3200]{2,1,0:T(8,128)(2,1)}), bf16[8,32,3200]{2,1,0:T(8,128)(2,1)S(1)}, u32[]{:S(2)}, u32[]{:S(2)}) %all-to-all-start.1) | async-done | bytes 1638432 | tf_op jit(solution)/shard_map/all_to_all | solution.py:349
  101.6 0.8 multiply_bitcast_fusion
  (65 shorter events, 3.4 us)
Async XLA Ops:
  0.6 9.3 %copy-start = (f32[1,4,8,3200]{3,2,1,0:T(8,128)S(1)}, f32[1,4,8,3200]{3,2,1,0:T(8,128)}, u32[]{:S(2)}) copy-start(f32[1,4,8,3200]{3,2,1,0:T(8,128)} %param.11) | copy-start | bytes 1228804
  0.6 18.3 %copy-start.17 = (s32[1,16]{1,0:T(1,128)S(1)}, s32[1,16]{1,0:T(1,128)}, u32[]{:S(2)}) copy-start(s32[1,16]{1,0:T(1,128)} %param.9) | copy-start | bytes 196
  1.8 42.0 %copy-start.2 = (bf16[9,32,1024]{2,1,0:T(8,128)(2,1)}, bf16[9,32,1024]{2,1,0:T(8,128)(2,1)S(1)}, u32[]{:S(2)}) copy-start(bf16[9,32,1024]{2,1,0:T(8,128)(2,1)S(1)} %slice.27.own.rest_0_) | copy-start | bytes 1769476
  1.8 28.4 %collective-permute-start.1 = (bf16[9,32,1024]{2,1,0:T(8,128)(2,1)S(1)}, bf16[9,32,1024]{2,1,0:T(8,128)(2,1)}, u32[]{:S(2)}, u32[]{:S(2)}) collective-permute-start(bf16[9,32,1024]{2,1,0:T(8,128)(2,1)S(1)} %slice.27.own.rest_0_), channel_id=1, source_target_pairs={{0,1},{1,2},{2,3},{3,0},{4,5},{5,6},{6,7},{7,4},{8,9},{9,10},{10,1... | collective-permute-start | bytes 1769480 | tf_op jit(solution)/shard_map/ppermute | solution.py:325
  4.0 26.3 %collective-permute-start = (bf16[9,32,1024]{2,1,0:T(8,128)(2,1)S(1)}, bf16[9,32,1024]{2,1,0:T(8,128)(2,1)}, u32[]{:S(2)}, u32[]{:S(2)}) collective-permute-start(bf16[9,32,1024]{2,1,0:T(8,128)(2,1)S(1)} %slice.27.own.rest_0_), channel_id=1, source_target_pairs={{0,3},{1,0},{2,1},{3,2},{4,7},{5,4},{6,5},{7,6},{8,11},{9,8},{10,9... | collective-permute-start | bytes 1769480 | tf_op jit(solution)/shard_map/ppermute | solution.py:324
  6.5 52.9 %copy-start.1 = (bf16[9,32,1280]{2,1,0:T(8,128)(2,1)}, bf16[9,32,1280]{2,1,0:T(8,128)(2,1)S(1)}, u32[]{:S(2)}) copy-start(bf16[9,32,1280]{2,1,0:T(8,128)(2,1)S(1)} %slice.30.own.rest_5_) | copy-start | bytes 2211844
  6.5 29.9 %collective-permute-start.5 = (bf16[9,32,1280]{2,1,0:T(8,128)(2,1)S(1)}, bf16[9,32,1280]{2,1,0:T(8,128)(2,1)}, u32[]{:S(2)}, u32[]{:S(2)}) collective-permute-start(bf16[9,32,1280]{2,1,0:T(8,128)(2,1)S(1)} %slice.30.own.rest_5_), channel_id=1, source_target_pairs={{0,1},{1,2},{2,3},{3,0},{4,5},{5,6},{6,7},{7,4},{8,9},{9,10},{10,1... | collective-permute-start | bytes 2211848 | tf_op jit(solution)/shard_map/ppermute | solution.py:325
  6.7 32.4 %collective-permute-start.4 = (bf16[9,32,1280]{2,1,0:T(8,128)(2,1)S(1)}, bf16[9,32,1280]{2,1,0:T(8,128)(2,1)S(1)}, u32[]{:S(2)}, u32[]{:S(2)}) collective-permute-start(bf16[9,32,1280]{2,1,0:T(8,128)(2,1)S(1)} %slice.30.own.rest_5_), channel_id=1, source_target_pairs={{0,3},{1,0},{2,1},{3,2},{4,7},{5,4},{6,5},{7,6},{8,11},{9,8},{10,9... | collective-permute-start | bytes 2211848 | tf_op jit(solution)/shard_map/ppermute | solution.py:324
  10.6 19.6 %all-to-all-start = ((bf16[4,4,8,640]{3,2,1,0:T(8,128)(2,1)}), bf16[4,4,8,640]{3,2,1,0:T(8,128)(2,1)S(1)}, u32[]{:S(2)}, u32[]{:S(2)}) async-start(bf16[4,4,8,640]{3,2,1,0:T(8,128)(2,1)} %broadcast_in_dim.9), calls=%async_computation | async-start | bytes 327680 | tf_op jit(solution)/shard_map/all_to_all | solution.py:357
  30.2 11.7 %copy-start.15 = (bf16[4,4,8,640]{3,2,1,0:T(8,128)(2,1)}, bf16[4,4,8,640]{3,2,1,0:T(8,128)(2,1)S(1)}, u32[]{:S(2)}) copy-start(bf16[4,4,8,640]{3,2,1,0:T(8,128)(2,1)S(1)} %all-to-all-done) | copy-start | bytes 491524
  30.3 13.5 %copy-start.7 = (s32[18]{0:T(128)S(1)}, s32[18]{0:T(128)}, u32[]{:S(2)}) copy-start(s32[18]{0:T(128)} %stack.71.scal) | copy-start | bytes 220
  30.3 13.5 %copy-start.14 = (bf16[512,1152]{1,0:T(8,128)(2,1)S(1)}, bf16[512,1152]{1,0:T(8,128)(2,1)}, u32[]{:S(2)}) copy-start(bf16[512,1152]{1,0:T(8,128)(2,1)} %get-tuple-element.71.ctx) | copy-start | bytes 3538948
  31.4 8.4 %collective-permute-start.3 = (bf16[5,32,1024]{2,1,0:T(8,128)(2,1)S(1)}, bf16[5,32,1024]{2,1,0:T(8,128)(2,1)S(1)}, u32[]{:S(2)}, u32[]{:S(2)}) collective-permute-start(bf16[5,32,1024]{2,1,0:T(8,128)(2,1)S(1)} %slice.29), channel_id=1, source_target_pairs={{0,1},{1,2},{2,3},{3,0},{4,5},{5,6},{6,7},{7,4},{8,9},{9,10},{10,1... | collective-permute-start | bytes 983048 | tf_op jit(solution)/shard_map/ppermute | solution.py:333
  32.4 6.6 %collective-permute-start.2 = (bf16[4,32,1024]{2,1,0:T(8,128)(2,1)S(1)}, bf16[4,32,1024]{2,1,0:T(8,128)(2,1)S(1)}, u32[]{:S(2)}, u32[]{:S(2)}) collective-permute-start(bf16[4,32,1024]{2,1,0:T(8,128)(2,1)S(1)} %slice.28), channel_id=1, source_target_pairs={{0,3},{1,0},{2,1},{3,2},{4,7},{5,4},{6,5},{7,6},{8,11},{9,8},{10,9... | collective-permute-start | bytes 786440 | tf_op jit(solution)/shard_map/ppermute | solution.py:332
  36.3 32.1 %copy-start.3 = (bf16[9,32,896]{2,1,0:T(8,128)(2,1)}, bf16[9,32,896]{2,1,0:T(8,128)(2,1)S(1)}, u32[]{:S(2)}) copy-start(bf16[9,32,896]{2,1,0:T(8,128)(2,1)S(1)} %slice.33.own.rest_10_) | copy-start | bytes 1548292
  36.3 15.1 %collective-permute-start.9 = (bf16[9,32,896]{2,1,0:T(8,128)(2,1)S(1)}, bf16[9,32,896]{2,1,0:T(8,128)(2,1)S(1)}, u32[]{:S(2)}, u32[]{:S(2)}) collective-permute-start(bf16[9,32,896]{2,1,0:T(8,128)(2,1)S(1)} %slice.33.own.rest_10_), channel_id=1, source_target_pairs={{0,1},{1,2},{2,3},{3,0},{4,5},{5,6},{6,7},{7,4},{8,9},{9,10},{10,1... | collective-permute-start | bytes 1548296 | tf_op jit(solution)/shard_map/ppermute | solution.py:325
  36.4 15.0 %collective-permute-start.8 = (bf16[9,32,896]{2,1,0:T(8,128)(2,1)S(1)}, bf16[9,32,896]{2,1,0:T(8,128)(2,1)S(1)}, u32[]{:S(2)}, u32[]{:S(2)}) collective-permute-start(bf16[9,32,896]{2,1,0:T(8,128)(2,1)S(1)} %slice.33.own.rest_10_), channel_id=1, source_target_pairs={{0,3},{1,0},{2,1},{3,2},{4,7},{5,4},{6,5},{7,6},{8,11},{9,8},{10,9... | collective-permute-start | bytes 1548296 | tf_op jit(solution)/shard_map/ppermute | solution.py:324
  39.0 20.3 %copy-start.4 = (bf16[9,32,1280]{2,1,0:T(8,128)(2,1)}, bf16[9,32,1280]{2,1,0:T(8,128)(2,1)S(1)}, u32[]{:S(2)}) copy-start(bf16[9,32,1280]{2,1,0:T(8,128)(2,1)S(1)} %collective-permute-done.4.plus1.rest_6_) | copy-start | bytes 2211844
  39.0 8.9 %copy-start.12 = (bf16[4,32,1024]{2,1,0:T(8,128)(2,1)}, bf16[4,32,1024]{2,1,0:T(8,128)(2,1)S(1)}, u32[]{:S(2)}) copy-start(bf16[4,32,1024]{2,1,0:T(8,128)(2,1)S(1)} %collective-permute-done.2.plus2_low.rest_2_) | copy-start | bytes 786436
  39.8 8.2 %copy-start.9 = (bf16[5,32,1024]{2,1,0:T(8,128)(2,1)}, bf16[5,32,1024]{2,1,0:T(8,128)(2,1)S(1)}, u32[]{:S(2)}) copy-start(bf16[5,32,1024]{2,1,0:T(8,128)(2,1)S(1)} %collective-permute-done.3.plus2_high.rest_3_) | copy-start | bytes 983044
  40.9 17.8 %collective-permute-start.7 = (bf16[4,32,1280]{2,1,0:T(8,128)(2,1)S(1)}, bf16[4,32,1280]{2,1,0:T(8,128)(2,1)S(1)}, u32[]{:S(2)}, u32[]{:S(2)}) collective-permute-start(bf16[4,32,1280]{2,1,0:T(8,128)(2,1)S(1)} %slice.32), channel_id=1, source_target_pairs={{0,1},{1,2},{2,3},{3,0},{4,5},{5,6},{6,7},{7,4},{8,9},{9,10},{10,1... | collective-permute-start | bytes 983048 | tf_op jit(solution)/shard_map/ppermute | solution.py:333
  42.0 17.4 %collective-permute-start.6 = (bf16[5,32,1280]{2,1,0:T(8,128)(2,1)S(1)}, bf16[5,32,1280]{2,1,0:T(8,128)(2,1)S(1)}, u32[]{:S(2)}, u32[]{:S(2)}) collective-permute-start(bf16[5,32,1280]{2,1,0:T(8,128)(2,1)S(1)} %slice.31), channel_id=1, source_target_pairs={{0,3},{1,0},{2,1},{3,2},{4,7},{5,4},{6,5},{7,6},{8,11},{9,8},{10,9... | collective-permute-start | bytes 1228808 | tf_op jit(solution)/shard_map/ppermute | solution.py:332
  51.4 17.0 %copy-start.5 = (bf16[9,32,896]{2,1,0:T(8,128)(2,1)}, bf16[9,32,896]{2,1,0:T(8,128)(2,1)S(1)}, u32[]{:S(2)}) copy-start(bf16[9,32,896]{2,1,0:T(8,128)(2,1)S(1)} %collective-permute-done.9.minus1.rest_14_) | copy-start | bytes 1548292
  51.4 17.0 %copy-start.6 = (bf16[9,32,896]{2,1,0:T(8,128)(2,1)}, bf16[9,32,896]{2,1,0:T(8,128)(2,1)S(1)}, u32[]{:S(2)}) copy-start(bf16[9,32,896]{2,1,0:T(8,128)(2,1)S(1)} %collective-permute-done.8.plus1.rest_11_) | copy-start | bytes 1548292
  51.4 12.9 %collective-permute-start.11 = (bf16[4,32,896]{2,1,0:T(8,128)(2,1)S(1)}, bf16[4,32,896]{2,1,0:T(8,128)(2,1)S(1)}, u32[]{:S(2)}, u32[]{:S(2)}) collective-permute-start(bf16[4,32,896]{2,1,0:T(8,128)(2,1)S(1)} %slice.34), channel_id=1, source_target_pairs={{0,3},{1,0},{2,1},{3,2},{4,7},{5,4},{6,5},{7,6},{8,11},{9,8},{10,9... | collective-permute-start | bytes 688136 | tf_op jit(solution)/shard_map/ppermute | solution.py:332
  54.1 10.2 %collective-permute-start.12 = (bf16[5,32,896]{2,1,0:T(8,128)(2,1)S(1)}, bf16[5,32,896]{2,1,0:T(8,128)(2,1)S(1)}, u32[]{:S(2)}, u32[]{:S(2)}) collective-permute-start(bf16[5,32,896]{2,1,0:T(8,128)(2,1)S(1)} %slice.35), channel_id=1, source_target_pairs={{0,1},{1,2},{2,3},{3,0},{4,5},{5,6},{6,7},{7,4},{8,9},{9,10},{10,1... | collective-permute-start | bytes 860168 | tf_op jit(solution)/shard_map/ppermute | solution.py:333
  54.2 10.1 %collective-permute-start.10 = (bf16[8,32,1024]{2,1,0:T(8,128)(2,1)S(1)}, bf16[8,32,1024]{2,1,0:T(8,128)(2,1)S(1)}, u32[]{:S(2)}, u32[]{:S(2)}) collective-permute-start(bf16[8,32,1024]{2,1,0:T(8,128)(2,1)S(1)} %get-tuple-element.59), channel_id=1, source_target_pairs={{0,4},{4,0},{8,12},{12,8},{16,20},{20,16},{24,28},{28,24},{32,36},... | collective-permute-start | bytes 1572872 | tf_op jit(solution)/shard_map/ppermute | solution.py:344
  64.3 7.3 %copy-start.13 = (bf16[4,32,896]{2,1,0:T(8,128)(2,1)}, bf16[4,32,896]{2,1,0:T(8,128)(2,1)S(1)}, u32[]{:S(2)}) copy-start(bf16[4,32,896]{2,1,0:T(8,128)(2,1)S(1)} %collective-permute-done.11.plus2_low.rest_12_) | copy-start | bytes 688132
  64.3 7.3 %copy-start.11 = (bf16[5,32,896]{2,1,0:T(8,128)(2,1)}, bf16[5,32,896]{2,1,0:T(8,128)(2,1)S(1)}, u32[]{:S(2)}) copy-start(bf16[5,32,896]{2,1,0:T(8,128)(2,1)S(1)} %collective-permute-done.12.plus2_high.rest_13_) | copy-start | bytes 860164
  64.3 7.3 %collective-permute-start.13 = (bf16[8,32,1280]{2,1,0:T(8,128)(2,1)S(1)}, bf16[8,32,1280]{2,1,0:T(8,128)(2,1)S(1)}, u32[]{:S(2)}, u32[]{:S(2)}) collective-permute-start(bf16[8,32,1280]{2,1,0:T(8,128)(2,1)S(1)} %get-tuple-element.66), channel_id=1, source_target_pairs={{0,4},{4,0},{8,12},{12,8},{16,20},{20,16},{24,28},{28,24},{32,36},... | collective-permute-start | bytes 1966088 | tf_op jit(solution)/shard_map/ppermute | solution.py:344
  71.6 1.9 %collective-permute-start.14 = (bf16[8,32,896]{2,1,0:T(8,128)(2,1)S(1)}, bf16[8,32,896]{2,1,0:T(8,128)(2,1)S(1)}, u32[]{:S(2)}, u32[]{:S(2)}) collective-permute-start(bf16[8,32,896]{2,1,0:T(8,128)(2,1)S(1)} %get-tuple-element.83), channel_id=1, source_target_pairs={{0,4},{4,0},{8,12},{12,8},{16,20},{20,16},{24,28},{28,24},{32,36},... | collective-permute-start | bytes 1376264 | tf_op jit(solution)/shard_map/ppermute | solution.py:344
  75.0 26.4 %all-to-all-start.1 = ((bf16[8,32,3200]{2,1,0:T(8,128)(2,1)}), bf16[8,32,3200]{2,1,0:T(8,128)(2,1)S(1)}, u32[]{:S(2)}, u32[]{:S(2)}) async-start(bf16[8,32,3200]{2,1,0:T(8,128)(2,1)} %pad_maximum_fusion), calls=%async_computation.1 | async-start | bytes 3276800 | tf_op jit(solution)/shard_map/all_to_all | solution.py:349
  (3 other events, 15.6 us)

commit v3 on v2

--- a/solution.py
+++ b/solution.py
@@ -343,11 +343,6 @@
     def cross_core(i):
         st[f"core{i}"] = lax.ppermute(st[f"send{i}"], "dp", flip_core())
 
-    def cross_chips(*some):
-        both = [(st[f"keep{i}"].astype(F32) + st[f"core{i}"].astype(F32)).astype(BF16) for i in some]
-        both = jnp.concatenate(both, axis=2)
-        return lax.all_to_all(both, "dp", 0, 0, axis_index_groups=same_core, tiled=True)
-
     send_own(0)
     send_own(1)
     qkv, probs, st["ctx"] = forward(scal, projections)
@@ -371,7 +366,12 @@
     sum_chunk(2)
     fence("keep0", "core0", "keep1", "core1", "keep2", "send2", "far2")
     cross_core(2)
-    summed = [cross_chips(0, 1, 2)]
+    early = [(st[f"keep{i}"].astype(F32) + st[f"core{i}"].astype(F32)).astype(BF16) for i in (0, 1)]
+    st["sums"] = jnp.concatenate(early + [jnp.zeros_like(st["keep2"])], axis=2)
+    fence("sums", "keep2", "core2")
+    late = (st["keep2"].astype(F32) + st["core2"].astype(F32)).astype(BF16)
+    sums = lax.dynamic_update_slice(st["sums"], late, (0, 0, cuts[2][0]))
+    summed = [lax.all_to_all(sums, "dp", 0, 0, axis_index_groups=same_core, tiled=True)]
     ctx_grad = context_gradient(scal, weight, [pieces(i) for i in range(n)], cuts)
     gradients = backward(scal, ctx_grad, qkv, probs)
     weight_grad = jnp.concatenate([jnp.sum(p.astype(F32), axis=0) for p in summed], axis=1) / (CAP * dp_size)

time: 103 us -> 102 us (level)
  waiting for transfers between devices: 11.4 us -> 10.1 us
    ppermute x3, waiting for transfers between devices: 1.41 us -> 0.01 us  [cross_core(): st[f'core{i}'] = lax.ppermute(st[f'send{i}'], 'dp', flip_core())]
  transfers between devices with their start and end apart: 17 -> 17, of which waited for: 5 -> 4; matrix products, arithmetic and copies ran while one was open for 9% -> 10% of each run, Pallas kernels for 36% -> 37%
where the time goes in v3:
time: 102 us
  starting transfers between devices  39.3 us (39%)
  Pallas kernels  37.2 us (36%)
  waiting for transfers between devices  10.1 us (10%)
  local copies, waits for them, and re-layouts  9.31 us (9%)
  other arithmetic  4.33 us (4%)
  between operations  1.62 us (2%)
    pallas_call x3, Pallas kernels, weight_sums(): pl.pallas_call(sums_kernel, in_specs=[pl.BlockSpec(memory_space=pltpu.SME...  12.3 us
    pallas_call x1, Pallas kernels, forward(): pl.pallas_call(forward_kernel, grid_spec=pltpu.PrefetchScalarGridSpec(num...  9.49 us
    ppermute x3, starting transfers between devices, cross_core(): st[f'core{i}'] = lax.ppermute(st[f'send{i}'], 'dp', flip_core())  8.54 us
    all_to_all x1, starting transfers between devices, body(): st['drift'] = lax.all_to_all(every, 'rep', 0, 0, tiled=True)  8.29 us
    pallas_call x1, Pallas kernels, context_gradient(): pl.pallas_call(functools.partial(ctx_grad_kernel, groups, cuts), in_specs...  8.27 us
    pallas_call x1, Pallas kernels, backward(): pl.pallas_call(backward_kernel, in_specs=[pl.BlockSpec(memory_space=pltpu...  7.19 us
    ppermute x3, starting transfers between devices, pass_on(): lax.ppermute(plus1[:split], 'fsdp', shift_x(-1))  7.08 us
    ppermute x3, starting transfers between devices, send_own(): lax.ppermute(st[f'own{i}'], 'fsdp', shift_x(-1))  6.58 us
  transfers between devices with their start and end apart: 17, of which 4 were waited for; matrix products, arithmetic and copies ran while one was open for 10% of the time, Pallas kernels for 37%

profile of v3, /device:TPU:1, one launch (start us, length us, event | category | flops | bytes accessed | tf_op | source)
XLA Modules:
  0.0 101.8 jit_solution(14353820926077949404)
XLA Ops:
  0.7 1.2 %slice.27.own.rest_0_ = bf16[9,32,1024]{2,1,0:T(8,128)(2,1)S(1)} slice(bf16[9,32,3200]{2,1,0:T(8,128)(2,1)} %param.7), slice={[0:9], [0:32], [0:1024]} | slice | bytes 1179648 | tf_op jit(solution)/shard_map/slice | solution.py:322
  1.8 2.1 %collective-permute-start.1 = (bf16[9,32,1024]{2,1,0:T(8,128)(2,1)S(1)}, bf16[9,32,1024]{2,1,0:T(8,128)(2,1)}, u32[]{:S(2)}, u32[]{:S(2)}) collective-permute-start(bf16[9,32,1024]{2,1,0:T(8,128)(2,1)S(1)} %slice.27.own.rest_0_), channel_id=1, source_target_pairs={{0,1},{1,2},{2,3},{3,0},{4,5},{5,6},{6,7},{7,4},{8,9},{9,10},{10,1... | collective-permute-start | bytes 1769480 | tf_op jit(solution)/shard_map/ppermute | solution.py:325
  4.0 1.4 %collective-permute-start = (bf16[9,32,1024]{2,1,0:T(8,128)(2,1)S(1)}, bf16[9,32,1024]{2,1,0:T(8,128)(2,1)}, u32[]{:S(2)}, u32[]{:S(2)}) collective-permute-start(bf16[9,32,1024]{2,1,0:T(8,128)(2,1)S(1)} %slice.27.own.rest_0_), channel_id=1, source_target_pairs={{0,3},{1,0},{2,1},{3,2},{4,7},{5,4},{6,5},{7,6},{8,11},{9,8},{10,9... | collective-permute-start | bytes 1769480 | tf_op jit(solution)/shard_map/ppermute | solution.py:324
  5.3 1.2 %slice.30.own.rest_5_ = bf16[9,32,1280]{2,1,0:T(8,128)(2,1)S(1)} slice(bf16[9,32,3200]{2,1,0:T(8,128)(2,1)} %param.7), slice={[0:9], [0:32], [1024:2304]} | slice | bytes 1474560 | tf_op jit(solution)/shard_map/slice | solution.py:322
  6.7 2.6 %collective-permute-start.4 = (bf16[9,32,1280]{2,1,0:T(8,128)(2,1)S(1)}, bf16[9,32,1280]{2,1,0:T(8,128)(2,1)S(1)}, u32[]{:S(2)}, u32[]{:S(2)}) collective-permute-start(bf16[9,32,1280]{2,1,0:T(8,128)(2,1)S(1)} %slice.30.own.rest_5_), channel_id=1, source_target_pairs={{0,3},{1,0},{2,1},{3,2},{4,7},{5,4},{6,5},{7,6},{8,11},{9,8},{10,9... | collective-permute-start | bytes 2211848 | tf_op jit(solution)/shard_map/ppermute | solution.py:324
  10.6 8.3 %all-to-all-start = ((bf16[4,4,8,640]{3,2,1,0:T(8,128)(2,1)}), bf16[4,4,8,640]{3,2,1,0:T(8,128)(2,1)S(1)}, u32[]{:S(2)}, u32[]{:S(2)}) async-start(bf16[4,4,8,640]{3,2,1,0:T(8,128)(2,1)} %broadcast_in_dim.12), calls=%async_computation | async-start | bytes 327680 | tf_op jit(solution)/shard_map/all_to_all | solution.py:352
  19.5 1.3 %stack.71.scal = s32[18]{0:T(128)} concatenate(s32[1]{0:T(128)} %bitcast, s32[1]{0:T(128)} %bitcast.1, s32[1]{0:T(128)} %bitcast.2, s32[1]{0:T(128)} %bitcast.3, s32[1]{0:T(128)} %bitcast.4, s32[1]{0:T(128)} %bitcast.5, s32[1]{0:T(128)} %bitcast.6, s32[1]{0:T(128)} %bitcast.7, s32[1]{0:T(128)} %bitcast.8, s32[1]{0:T(128)} %bitcast.9, s32[1]{0:T(128)} %bitcast.10, s32[1]{0:T(128)} %bitcast.11, ...), dimensions={0} | concatenate | bytes 144 | tf_op jit(solution)/shard_map/stack | solution.py:309
  20.8 9.5 %forward.1 = (bf16[9,4,128,384]{3,2,1,0:T(8,128)(2,1)}, f32[9,4,128,128]{3,2,1,0:T(8,128)}, bf16[512,1152]{1,0:T(8,128)(2,1)}) custom-call(s32[18]{0:T(128)} %stack.71.scal, bf16[9,128,4,384]{3,2,1,0:T(4,128)(2,1)} %proj.1), custom_call_target="tpu_custom_call" | custom-call | flops 1207959552 | bytes 12000000 | tf_op jit(solution)/shard_map/forward/pallas_call | solution.py:56
  30.3 1.0 slice.29
  31.4 1.0 %slice.28 = bf16[4,32,1024]{2,1,0:T(8,128)(2,1)S(1)} slice(bf16[9,32,1024]{2,1,0:T(8,128)(2,1)} %collective-permute-done.plus1.rest_1_), slice={[0:4], [0:32], [0:1024]} | slice | bytes 524288 | tf_op jit(solution)/shard_map/slice | solution.py:332
  32.5 2.7 %collective-permute-start.2 = (bf16[4,32,1024]{2,1,0:T(8,128)(2,1)S(1)}, bf16[4,32,1024]{2,1,0:T(8,128)(2,1)S(1)}, u32[]{:S(2)}, u32[]{:S(2)}) collective-permute-start(bf16[4,32,1024]{2,1,0:T(8,128)(2,1)S(1)} %slice.28), channel_id=1, source_target_pairs={{0,3},{1,0},{2,1},{3,2},{4,7},{5,4},{6,5},{7,6},{8,11},{9,8},{10,9... | collective-permute-start | bytes 786440 | tf_op jit(solution)/shard_map/ppermute | solution.py:332
  35.1 1.1 %slice.33.own.rest_10_ = bf16[9,32,896]{2,1,0:T(8,128)(2,1)S(1)} slice(bf16[9,32,3200]{2,1,0:T(8,128)(2,1)} %param.7), slice={[0:9], [0:32], [2304:3200]} | slice | bytes 1032192 | tf_op jit(solution)/shard_map/slice | solution.py:322
  36.3 2.7 %collective-permute-start.8 = (bf16[9,32,896]{2,1,0:T(8,128)(2,1)S(1)}, bf16[9,32,896]{2,1,0:T(8,128)(2,1)S(1)}, u32[]{:S(2)}, u32[]{:S(2)}) collective-permute-start(bf16[9,32,896]{2,1,0:T(8,128)(2,1)S(1)} %slice.33.own.rest_10_), channel_id=1, source_target_pairs={{0,3},{1,0},{2,1},{3,2},{4,7},{5,4},{6,5},{7,6},{8,11},{9,8},{10,9... | collective-permute-start | bytes 1548296 | tf_op jit(solution)/shard_map/ppermute | solution.py:324
  39.0 0.7 collective-permute-done.3.plus2_high.rest_3_
  39.8 1.1 %slice.32 = bf16[4,32,1280]{2,1,0:T(8,128)(2,1)S(1)} slice(bf16[9,32,1280]{2,1,0:T(8,128)(2,1)} %collective-permute-done.5.minus1.rest_9_), slice={[5:9], [0:32], [0:1280]} | slice | bytes 655360 | tf_op jit(solution)/shard_map/slice | solution.py:333
  40.9 1.1 %collective-permute-start.7 = (bf16[4,32,1280]{2,1,0:T(8,128)(2,1)S(1)}, bf16[4,32,1280]{2,1,0:T(8,128)(2,1)S(1)}, u32[]{:S(2)}, u32[]{:S(2)}) collective-permute-start(bf16[4,32,1280]{2,1,0:T(8,128)(2,1)S(1)} %slice.32), channel_id=1, source_target_pairs={{0,1},{1,2},{2,3},{3,0},{4,5},{5,6},{6,7},{7,4},{8,9},{9,10},{10,1... | collective-permute-start | bytes 983048 | tf_op jit(solution)/shard_map/ppermute | solution.py:333
  42.0 1.7 %collective-permute-start.6 = (bf16[5,32,1280]{2,1,0:T(8,128)(2,1)S(1)}, bf16[5,32,1280]{2,1,0:T(8,128)(2,1)S(1)}, u32[]{:S(2)}, u32[]{:S(2)}) collective-permute-start(bf16[5,32,1280]{2,1,0:T(8,128)(2,1)S(1)} %slice.31), channel_id=1, source_target_pairs={{0,3},{1,0},{2,1},{3,2},{4,7},{5,4},{6,5},{7,6},{8,11},{9,8},{10,9... | collective-permute-start | bytes 1228808 | tf_op jit(solution)/shard_map/ppermute | solution.py:332
  43.7 4.1 %weight_sums.3 = (bf16[8,32,1024]{2,1,0:T(8,128)(2,1)S(1)}, bf16[8,32,1024]{2,1,0:T(8,128)(2,1)S(1)}) custom-call(s32[18]{0:T(128)S(1)} %copy-done.7, bf16[9,32,1024]{2,1,0:T(8,128)(2,1)S(1)} %slice.27.own.rest_0_, bf16[9,32,1024]{2,1,0:T(8,128)(2,1)} %collective-permute-done.plus1.rest_1_, ...), custom_call_target="tpu_custom_call" | custom-call | flops 8000000000 | bytes 1000 | tf_op jit(solution)/shard_map/weight_sums/pallas_call | solution.py:142
  47.9 3.5 %collective-permute-done.9.minus1.rest_14_ = bf16[9,32,896]{2,1,0:T(8,128)(2,1)S(1)} collective-permute-done((bf16[9,32,896]{2,1,0:T(8,128)(2,1)S(1)}, bf16[9,32,896]{2,1,0:T(8,128)(2,1)S(1)}, u32[]{:S(2)}, u32[]{:S(2)}) %collective-permute-start.9) | collective-permute-done | bytes 516128 | tf_op jit(solution)/shard_map/ppermute | solution.py:325
  51.4 2.7 %collective-permute-start.11 = (bf16[4,32,896]{2,1,0:T(8,128)(2,1)S(1)}, bf16[4,32,896]{2,1,0:T(8,128)(2,1)S(1)}, u32[]{:S(2)}, u32[]{:S(2)}) collective-permute-start(bf16[4,32,896]{2,1,0:T(8,128)(2,1)S(1)} %slice.34), channel_id=1, source_target_pairs={{0,3},{1,0},{2,1},{3,2},{4,7},{5,4},{6,5},{7,6},{8,11},{9,8},{10,9... | collective-permute-start | bytes 688136 | tf_op jit(solution)/shard_map/ppermute | solution.py:332
  54.2 4.4 %collective-permute-start.10 = (bf16[8,32,1024]{2,1,0:T(8,128)(2,1)S(1)}, bf16[8,32,1024]{2,1,0:T(8,128)(2,1)S(1)}, u32[]{:S(2)}, u32[]{:S(2)}) collective-permute-start(bf16[8,32,1024]{2,1,0:T(8,128)(2,1)S(1)} %get-tuple-element.62), channel_id=1, source_target_pairs={{0,4},{4,0},{8,12},{12,8},{16,20},{20,16},{24,28},{28,24},{32,36},... | collective-permute-start | bytes 1572872 | tf_op jit(solution)/shard_map/ppermute | solution.py:344
  58.6 0.7 collective-permute-done.6.plus2_low.rest_7_
  59.4 4.9 %weight_sums.4 = (bf16[8,32,1280]{2,1,0:T(8,128)(2,1)S(1)}, bf16[8,32,1280]{2,1,0:T(8,128)(2,1)S(1)}) custom-call(s32[18]{0:T(128)S(1)} %copy-done.7, bf16[9,32,1280]{2,1,0:T(8,128)(2,1)S(1)} %slice.30.own.rest_5_, bf16[9,32,1280]{2,1,0:T(8,128)(2,1)S(1)} %collective-permute-done.4.plus1.rest_6_, ...), custom_call_target="tpu_custom_call" | custom-call | flops 8000000000 | bytes 1000 | tf_op jit(solution)/shard_map/weight_sums/pallas_call | solution.py:142
  64.3 4.0 %collective-permute-start.13 = (bf16[8,32,1280]{2,1,0:T(8,128)(2,1)S(1)}, bf16[8,32,1280]{2,1,0:T(8,128)(2,1)S(1)}, u32[]{:S(2)}, u32[]{:S(2)}) collective-permute-start(bf16[8,32,1280]{2,1,0:T(8,128)(2,1)S(1)} %get-tuple-element.69), channel_id=1, source_target_pairs={{0,4},{4,0},{8,12},{12,8},{16,20},{20,16},{24,28},{28,24},{32,36},... | collective-permute-start | bytes 1966088 | tf_op jit(solution)/shard_map/ppermute | solution.py:344
  68.3 3.3 %weight_sums.5 = (bf16[8,32,896]{2,1,0:T(8,128)(2,1)S(1)}, bf16[8,32,896]{2,1,0:T(8,128)(2,1)S(1)}) custom-call(s32[18]{0:T(128)S(1)} %copy-done.7, bf16[9,32,896]{2,1,0:T(8,128)(2,1)S(1)} %slice.33.own.rest_10_, bf16[9,32,896]{2,1,0:T(8,128)(2,1)S(1)} %collective-permute-done.8.plus1.rest_11_, ...), custom_call_target="tpu_custom_call" | custom-call | flops 8000000000 | bytes 1000 | tf_op jit(solution)/shard_map/weight_sums/pallas_call | solution.py:142
  72.1 1.4 %maximum_maximum_fusion = bf16[8,32,3200]{2,1,0:T(8,128)(2,1)} fusion(bf16[8,32,1280]{2,1,0:T(8,128)(2,1)S(1)} %add_convert_fusion, bf16[8,32,1024]{2,1,0:T(8,128)(2,1)S(1)} %add_convert_fusion.1, bf16[3200]{0:T(1024)(128)(2,1)S(1)} %pad.2.clone), kind=kLoop, calls=%fused_computation.1 | loop fusion | flops 4915200 | bytes 2824448 | tf_op jit(solution)/shard_map/concatenate | solution.py:370
  73.5 0.9 fusion
  74.4 5.1 %all-to-all-start.1 = ((bf16[8,32,3200]{2,1,0:T(8,128)(2,1)}), bf16[8,32,3200]{2,1,0:T(8,128)(2,1)S(1)}, u32[]{:S(2)}, u32[]{:S(2)}) async-start(bf16[8,32,3200]{2,1,0:T(8,128)(2,1)} %fusion), calls=%async_computation.1 | async-start | bytes 3276800 | tf_op jit(solution)/shard_map/all_to_all | solution.py:374
  80.2 8.3 %context_gradient.1.ctx_grad = bf16[1152,512]{1,0:T(8,128)(2,1)} custom-call(s32[18]{0:T(128)} %stack.71.scal, bf16[512,3200]{1,0:T(8,128)(2,1)} %bitcast.24, bf16[9,32,1024]{2,1,0:T(8,128)(2,1)} %copy-done.2, bf16[9,32,1024]{2,1,0:T(8,128)(2,1)} %collective-permute-done.plus1.rest_1_, bf16[4,32,1024]{2,1,0:T(8,128)(2,1)} %copy-done.12, ...), custom_call_target="tpu_custom_call" | custom-call | flops 8000000000 | bytes 1000 | tf_op jit(solution)/shard_map/context_gradient/pallas_call | solution.py:195
  88.5 7.2 %backward.1 = bf16[9,128,4,384]{3,2,1,0:T(4,128)(2,1)} custom-call(s32[18]{0:T(128)} %stack.71.scal, bf16[1152,512]{1,0:T(8,128)(2,1)} %context_gradient.1.ctx_grad, bf16[9,4,128,384]{3,2,1,0:T(8,128)(2,1)} %get-tuple-element.79.qkv, f32[9,4,128,128]{3,2,1,0:T(8,128)} %get-tuple-element.80.probs), custom_call_target="tpu_custom_call" | custom-call | flops 8000000000 | bytes 1000 | tf_op jit(solution)/shard_map/backward/pallas_call | solution.py:274
  95.7 5.1 %all-to-all-done.1 = bf16[8,32,3200]{2,1,0:T(8,128)(2,1)S(1)} async-done(((bf16[8,32,3200]{2,1,0:T(8,128)(2,1)}), bf16[8,32,3200]{2,1,0:T(8,128)(2,1)S(1)}, u32[]{:S(2)}, u32[]{:S(2)}) %all-to-all-start.1) | async-done | bytes 1638432 | tf_op jit(solution)/shard_map/all_to_all | solution.py:374
  101.0 0.8 multiply_bitcast_fusion
  (63 shorter events, 3.3 us)
Async XLA Ops:
  0.6 9.3 %copy-start = (f32[1,4,8,3200]{3,2,1,0:T(8,128)S(1)}, f32[1,4,8,3200]{3,2,1,0:T(8,128)}, u32[]{:S(2)}) copy-start(f32[1,4,8,3200]{3,2,1,0:T(8,128)} %param.11) | copy-start | bytes 1228804
  0.6 18.3 %copy-start.15 = (s32[1,16]{1,0:T(1,128)S(1)}, s32[1,16]{1,0:T(1,128)}, u32[]{:S(2)}) copy-start(s32[1,16]{1,0:T(1,128)} %param.9) | copy-start | bytes 196
  1.8 41.9 %copy-start.2 = (bf16[9,32,1024]{2,1,0:T(8,128)(2,1)}, bf16[9,32,1024]{2,1,0:T(8,128)(2,1)S(1)}, u32[]{:S(2)}) copy-start(bf16[9,32,1024]{2,1,0:T(8,128)(2,1)S(1)} %slice.27.own.rest_0_) | copy-start | bytes 1769476
  1.8 28.5 %collective-permute-start.1 = (bf16[9,32,1024]{2,1,0:T(8,128)(2,1)S(1)}, bf16[9,32,1024]{2,1,0:T(8,128)(2,1)}, u32[]{:S(2)}, u32[]{:S(2)}) collective-permute-start(bf16[9,32,1024]{2,1,0:T(8,128)(2,1)S(1)} %slice.27.own.rest_0_), channel_id=1, source_target_pairs={{0,1},{1,2},{2,3},{3,0},{4,5},{5,6},{6,7},{7,4},{8,9},{9,10},{10,1... | collective-permute-start | bytes 1769480 | tf_op jit(solution)/shard_map/ppermute | solution.py:325
  4.0 26.4 %collective-permute-start = (bf16[9,32,1024]{2,1,0:T(8,128)(2,1)S(1)}, bf16[9,32,1024]{2,1,0:T(8,128)(2,1)}, u32[]{:S(2)}, u32[]{:S(2)}) collective-permute-start(bf16[9,32,1024]{2,1,0:T(8,128)(2,1)S(1)} %slice.27.own.rest_0_), channel_id=1, source_target_pairs={{0,3},{1,0},{2,1},{3,2},{4,7},{5,4},{6,5},{7,6},{8,11},{9,8},{10,9... | collective-permute-start | bytes 1769480 | tf_op jit(solution)/shard_map/ppermute | solution.py:324
  6.5 52.9 %copy-start.1 = (bf16[9,32,1280]{2,1,0:T(8,128)(2,1)}, bf16[9,32,1280]{2,1,0:T(8,128)(2,1)S(1)}, u32[]{:S(2)}) copy-start(bf16[9,32,1280]{2,1,0:T(8,128)(2,1)S(1)} %slice.30.own.rest_5_) | copy-start | bytes 2211844
  6.5 29.8 %collective-permute-start.5 = (bf16[9,32,1280]{2,1,0:T(8,128)(2,1)S(1)}, bf16[9,32,1280]{2,1,0:T(8,128)(2,1)}, u32[]{:S(2)}, u32[]{:S(2)}) collective-permute-start(bf16[9,32,1280]{2,1,0:T(8,128)(2,1)S(1)} %slice.30.own.rest_5_), channel_id=1, source_target_pairs={{0,1},{1,2},{2,3},{3,0},{4,5},{5,6},{6,7},{7,4},{8,9},{9,10},{10,1... | collective-permute-start | bytes 2211848 | tf_op jit(solution)/shard_map/ppermute | solution.py:325
  6.7 32.3 %collective-permute-start.4 = (bf16[9,32,1280]{2,1,0:T(8,128)(2,1)S(1)}, bf16[9,32,1280]{2,1,0:T(8,128)(2,1)S(1)}, u32[]{:S(2)}, u32[]{:S(2)}) collective-permute-start(bf16[9,32,1280]{2,1,0:T(8,128)(2,1)S(1)} %slice.30.own.rest_5_), channel_id=1, source_target_pairs={{0,3},{1,0},{2,1},{3,2},{4,7},{5,4},{6,5},{7,6},{8,11},{9,8},{10,9... | collective-permute-start | bytes 2211848 | tf_op jit(solution)/shard_map/ppermute | solution.py:324
  10.6 19.7 %all-to-all-start = ((bf16[4,4,8,640]{3,2,1,0:T(8,128)(2,1)}), bf16[4,4,8,640]{3,2,1,0:T(8,128)(2,1)S(1)}, u32[]{:S(2)}, u32[]{:S(2)}) async-start(bf16[4,4,8,640]{3,2,1,0:T(8,128)(2,1)} %broadcast_in_dim.12), calls=%async_computation | async-start | bytes 327680 | tf_op jit(solution)/shard_map/all_to_all | solution.py:352
  31.3 12.4 %copy-start.7 = (s32[18]{0:T(128)S(1)}, s32[18]{0:T(128)}, u32[]{:S(2)}) copy-start(s32[18]{0:T(128)} %stack.71.scal) | copy-start | bytes 220
  31.3 12.4 %copy-start.14 = (bf16[512,1152]{1,0:T(8,128)(2,1)S(1)}, bf16[512,1152]{1,0:T(8,128)(2,1)}, u32[]{:S(2)}) copy-start(bf16[512,1152]{1,0:T(8,128)(2,1)} %get-tuple-element.74.ctx) | copy-start | bytes 3538948
  31.3 8.4 %collective-permute-start.3 = (bf16[5,32,1024]{2,1,0:T(8,128)(2,1)S(1)}, bf16[5,32,1024]{2,1,0:T(8,128)(2,1)S(1)}, u32[]{:S(2)}, u32[]{:S(2)}) collective-permute-start(bf16[5,32,1024]{2,1,0:T(8,128)(2,1)S(1)} %slice.29), channel_id=1, source_target_pairs={{0,1},{1,2},{2,3},{3,0},{4,5},{5,6},{6,7},{7,4},{8,9},{9,10},{10,1... | collective-permute-start | bytes 983048 | tf_op jit(solution)/shard_map/ppermute | solution.py:333
  32.5 6.5 %collective-permute-start.2 = (bf16[4,32,1024]{2,1,0:T(8,128)(2,1)S(1)}, bf16[4,32,1024]{2,1,0:T(8,128)(2,1)S(1)}, u32[]{:S(2)}, u32[]{:S(2)}) collective-permute-start(bf16[4,32,1024]{2,1,0:T(8,128)(2,1)S(1)} %slice.28), channel_id=1, source_target_pairs={{0,3},{1,0},{2,1},{3,2},{4,7},{5,4},{6,5},{7,6},{8,11},{9,8},{10,9... | collective-permute-start | bytes 786440 | tf_op jit(solution)/shard_map/ppermute | solution.py:332
  36.2 32.1 %copy-start.3 = (bf16[9,32,896]{2,1,0:T(8,128)(2,1)}, bf16[9,32,896]{2,1,0:T(8,128)(2,1)S(1)}, u32[]{:S(2)}) copy-start(bf16[9,32,896]{2,1,0:T(8,128)(2,1)S(1)} %slice.33.own.rest_10_) | copy-start | bytes 1548292
  36.2 15.1 %collective-permute-start.9 = (bf16[9,32,896]{2,1,0:T(8,128)(2,1)S(1)}, bf16[9,32,896]{2,1,0:T(8,128)(2,1)S(1)}, u32[]{:S(2)}, u32[]{:S(2)}) collective-permute-start(bf16[9,32,896]{2,1,0:T(8,128)(2,1)S(1)} %slice.33.own.rest_10_), channel_id=1, source_target_pairs={{0,1},{1,2},{2,3},{3,0},{4,5},{5,6},{6,7},{7,4},{8,9},{9,10},{10,1... | collective-permute-start | bytes 1548296 | tf_op jit(solution)/shard_map/ppermute | solution.py:325
  36.3 15.0 %collective-permute-start.8 = (bf16[9,32,896]{2,1,0:T(8,128)(2,1)S(1)}, bf16[9,32,896]{2,1,0:T(8,128)(2,1)S(1)}, u32[]{:S(2)}, u32[]{:S(2)}) collective-permute-start(bf16[9,32,896]{2,1,0:T(8,128)(2,1)S(1)} %slice.33.own.rest_10_), channel_id=1, source_target_pairs={{0,3},{1,0},{2,1},{3,2},{4,7},{5,4},{6,5},{7,6},{8,11},{9,8},{10,9... | collective-permute-start | bytes 1548296 | tf_op jit(solution)/shard_map/ppermute | solution.py:324
  39.0 20.4 %copy-start.4 = (bf16[9,32,1280]{2,1,0:T(8,128)(2,1)}, bf16[9,32,1280]{2,1,0:T(8,128)(2,1)S(1)}, u32[]{:S(2)}) copy-start(bf16[9,32,1280]{2,1,0:T(8,128)(2,1)S(1)} %collective-permute-done.4.plus1.rest_6_) | copy-start | bytes 2211844
  39.0 8.9 %copy-start.12 = (bf16[4,32,1024]{2,1,0:T(8,128)(2,1)}, bf16[4,32,1024]{2,1,0:T(8,128)(2,1)S(1)}, u32[]{:S(2)}) copy-start(bf16[4,32,1024]{2,1,0:T(8,128)(2,1)S(1)} %collective-permute-done.2.plus2_low.rest_2_) | copy-start | bytes 786436
  39.8 8.1 %copy-start.9 = (bf16[5,32,1024]{2,1,0:T(8,128)(2,1)}, bf16[5,32,1024]{2,1,0:T(8,128)(2,1)S(1)}, u32[]{:S(2)}) copy-start(bf16[5,32,1024]{2,1,0:T(8,128)(2,1)S(1)} %collective-permute-done.3.plus2_high.rest_3_) | copy-start | bytes 983044
  40.9 17.8 %collective-permute-start.7 = (bf16[4,32,1280]{2,1,0:T(8,128)(2,1)S(1)}, bf16[4,32,1280]{2,1,0:T(8,128)(2,1)S(1)}, u32[]{:S(2)}, u32[]{:S(2)}) collective-permute-start(bf16[4,32,1280]{2,1,0:T(8,128)(2,1)S(1)} %slice.32), channel_id=1, source_target_pairs={{0,1},{1,2},{2,3},{3,0},{4,5},{5,6},{6,7},{7,4},{8,9},{9,10},{10,1... | collective-permute-start | bytes 983048 | tf_op jit(solution)/shard_map/ppermute | solution.py:333
  42.0 17.3 %collective-permute-start.6 = (bf16[5,32,1280]{2,1,0:T(8,128)(2,1)S(1)}, bf16[5,32,1280]{2,1,0:T(8,128)(2,1)S(1)}, u32[]{:S(2)}, u32[]{:S(2)}) collective-permute-start(bf16[5,32,1280]{2,1,0:T(8,128)(2,1)S(1)} %slice.31), channel_id=1, source_target_pairs={{0,3},{1,0},{2,1},{3,2},{4,7},{5,4},{6,5},{7,6},{8,11},{9,8},{10,9... | collective-permute-start | bytes 1228808 | tf_op jit(solution)/shard_map/ppermute | solution.py:332
  51.4 16.9 %copy-start.5 = (bf16[9,32,896]{2,1,0:T(8,128)(2,1)}, bf16[9,32,896]{2,1,0:T(8,128)(2,1)S(1)}, u32[]{:S(2)}) copy-start(bf16[9,32,896]{2,1,0:T(8,128)(2,1)S(1)} %collective-permute-done.9.minus1.rest_14_) | copy-start | bytes 1548292
  51.4 16.9 %copy-start.6 = (bf16[9,32,896]{2,1,0:T(8,128)(2,1)}, bf16[9,32,896]{2,1,0:T(8,128)(2,1)S(1)}, u32[]{:S(2)}) copy-start(bf16[9,32,896]{2,1,0:T(8,128)(2,1)S(1)} %collective-permute-done.8.plus1.rest_11_) | copy-start | bytes 1548292
  51.4 12.9 %collective-permute-start.11 = (bf16[4,32,896]{2,1,0:T(8,128)(2,1)S(1)}, bf16[4,32,896]{2,1,0:T(8,128)(2,1)S(1)}, u32[]{:S(2)}, u32[]{:S(2)}) collective-permute-start(bf16[4,32,896]{2,1,0:T(8,128)(2,1)S(1)} %slice.34), channel_id=1, source_target_pairs={{0,3},{1,0},{2,1},{3,2},{4,7},{5,4},{6,5},{7,6},{8,11},{9,8},{10,9... | collective-permute-start | bytes 688136 | tf_op jit(solution)/shard_map/ppermute | solution.py:332
  54.1 10.2 %collective-permute-start.12 = (bf16[5,32,896]{2,1,0:T(8,128)(2,1)S(1)}, bf16[5,32,896]{2,1,0:T(8,128)(2,1)S(1)}, u32[]{:S(2)}, u32[]{:S(2)}) collective-permute-start(bf16[5,32,896]{2,1,0:T(8,128)(2,1)S(1)} %slice.35), channel_id=1, source_target_pairs={{0,1},{1,2},{2,3},{3,0},{4,5},{5,6},{6,7},{7,4},{8,9},{9,10},{10,1... | collective-permute-start | bytes 860168 | tf_op jit(solution)/shard_map/ppermute | solution.py:333
  54.2 10.1 %collective-permute-start.10 = (bf16[8,32,1024]{2,1,0:T(8,128)(2,1)S(1)}, bf16[8,32,1024]{2,1,0:T(8,128)(2,1)S(1)}, u32[]{:S(2)}, u32[]{:S(2)}) collective-permute-start(bf16[8,32,1024]{2,1,0:T(8,128)(2,1)S(1)} %get-tuple-element.62), channel_id=1, source_target_pairs={{0,4},{4,0},{8,12},{12,8},{16,20},{20,16},{24,28},{28,24},{32,36},... | collective-permute-start | bytes 1572872 | tf_op jit(solution)/shard_map/ppermute | solution.py:344
  58.6 5.6 %copy-start.10 = (bf16[4,32,1280]{2,1,0:T(8,128)(2,1)}, bf16[4,32,1280]{2,1,0:T(8,128)(2,1)S(1)}, u32[]{:S(2)}) copy-start(bf16[4,32,1280]{2,1,0:T(8,128)(2,1)S(1)} %collective-permute-done.7.plus2_high.rest_8_) | copy-start | bytes 983044
  64.3 7.3 %copy-start.13 = (bf16[4,32,896]{2,1,0:T(8,128)(2,1)}, bf16[4,32,896]{2,1,0:T(8,128)(2,1)S(1)}, u32[]{:S(2)}) copy-start(bf16[4,32,896]{2,1,0:T(8,128)(2,1)S(1)} %collective-permute-done.11.plus2_low.rest_12_) | copy-start | bytes 688132
  64.3 7.3 %copy-start.11 = (bf16[5,32,896]{2,1,0:T(8,128)(2,1)}, bf16[5,32,896]{2,1,0:T(8,128)(2,1)S(1)}, u32[]{:S(2)}) copy-start(bf16[5,32,896]{2,1,0:T(8,128)(2,1)S(1)} %collective-permute-done.12.plus2_high.rest_13_) | copy-start | bytes 860164
  64.3 7.3 %collective-permute-start.13 = (bf16[8,32,1280]{2,1,0:T(8,128)(2,1)S(1)}, bf16[8,32,1280]{2,1,0:T(8,128)(2,1)S(1)}, u32[]{:S(2)}, u32[]{:S(2)}) collective-permute-start(bf16[8,32,1280]{2,1,0:T(8,128)(2,1)S(1)} %get-tuple-element.69), channel_id=1, source_target_pairs={{0,4},{4,0},{8,12},{12,8},{16,20},{20,16},{24,28},{28,24},{32,36},... | collective-permute-start | bytes 1966088 | tf_op jit(solution)/shard_map/ppermute | solution.py:344
  71.6 1.9 %collective-permute-start.14 = (bf16[8,32,896]{2,1,0:T(8,128)(2,1)S(1)}, bf16[8,32,896]{2,1,0:T(8,128)(2,1)S(1)}, u32[]{:S(2)}, u32[]{:S(2)}) collective-permute-start(bf16[8,32,896]{2,1,0:T(8,128)(2,1)S(1)} %get-tuple-element.81), channel_id=1, source_target_pairs={{0,4},{4,0},{8,12},{12,8},{16,20},{20,16},{24,28},{28,24},{32,36},... | collective-permute-start | bytes 1376264 | tf_op jit(solution)/shard_map/ppermute | solution.py:344
  74.4 26.4 %all-to-all-start.1 = ((bf16[8,32,3200]{2,1,0:T(8,128)(2,1)}), bf16[8,32,3200]{2,1,0:T(8,128)(2,1)S(1)}, u32[]{:S(2)}, u32[]{:S(2)}) async-start(bf16[8,32,3200]{2,1,0:T(8,128)(2,1)} %fusion), calls=%async_computation.1 | async-start | bytes 3276800 | tf_op jit(solution)/shard_map/all_to_all | solution.py:374
  (1 other events, 4.9 us)
